TPU v7x, 32 devices: a whole 2x2x4 slice. The times are simulated.
32 devices in a mesh: dp: 8 (over y, x, core), seq: 4 (over z).
Axes of the slice: x: 2, y: 2, z: 4, core: 2. Of those that a mesh axis runs over, the one named last changes fastest.
Arguments:
- inputs: bfloat16 [16, 1024, 768], P('dp', 'seq'), may hold values from -6 to 6
- cotangent: bfloat16 [16, 1024, 768], P('dp', 'seq'), may hold values from -6 to 6
- time_table: bfloat16 [2000, 768], replicated, may hold values from -6 to 6
- timesteps: int32 [16], P('dp'), may hold values from 0 to 1999
- buckets: int32 [16], P('dp'), may hold values from 0 to 7
- mixer_weight: bfloat16 [768, 2304], replicated, may hold values from -0.3125 to 0.3125
- output_weight: bfloat16 [768, 768], replicated, may hold values from -0.75 to 0.75
- up_weight: bfloat16 [768, 3072], replicated, may hold values from -0.21875 to 0.21875
- down_weight: bfloat16 [3072, 768], replicated, may hold values from -0.109375 to 0.109375
- norm_gain: bfloat16 [2, 768], replicated, may hold values from 0.5 to 1.5
- norm_shift: bfloat16 [2, 768], replicated, may hold values from -3 to 3
- output_bias: bfloat16 [2, 768], replicated, may hold values from -3 to 3
- up_bias: bfloat16 [3072], replicated, may hold values from -4 to 4
Outputs:
- layer_out: bfloat16 [16, 1024, 768], P('dp', 'seq')
- input_grad: float32 [16, 1024, 768], P('dp', 'seq')
- mixer_grad: float32 [768, 2304], P('dp')
- output_grad: float32 [768, 768], P('dp')
- up_grad: float32 [768, 3072], P('dp')
- down_grad: float32 [3072, 768], P('dp')
- gain_grad: float32 [2, 768], replicated
- shift_grad: float32 [2, 768], replicated
- bias_grad: float32 [2, 768], replicated
- up_bias_grad: float32 [3072], replicated
- table_grad: float32 [2000, 768], P(None, 'dp')
- bucket_norms: float32 [8], replicated
- bucket_counts: float32 [8], replicated
All inputs are finite; a program needn't handle non-finite values.
Results may differ from a plain program's by a relative error of at most 0.012.
Values may be sent and summed in bfloat16 or wider, within the bound.
A program may use at most 192 MiB of HBM per device.

v0:
```python
import math

import jax
import jax.numpy as jnp
from jax import lax
from jax.sharding import PartitionSpec as P

HEADS = 12
HEAD_SIZE = 64
STEPS = 2000
BUCKETS = 8


EPS = 1e-05
HIGH = lax.Precision.HIGHEST


def contract_rows(left_side, right_side):
    return lax.dot_general(
        left_side, right_side, (((0,), (0,)), ((), ())), preferred_element_type=jnp.float32
    )


def contract_cols(left_side, right_side):
    return lax.dot_general(
        left_side, right_side, (((1,), (1,)), ((), ())), preferred_element_type=jnp.float32
    )


def exact_gelu(values):
    return jax.nn.gelu(values, approximate=False)


def normalize(values, gain_row, shift_row):
    centre = jnp.mean(values, axis=-1, keepdims=True)
    centred = values - centre
    spread = jnp.mean(centred * centred, axis=-1, keepdims=True)
    inverse = lax.rsqrt(spread + EPS)
    unit_rows = centred * inverse
    return (unit_rows * gain_row + shift_row, unit_rows, inverse)


def normalize_back(grad_out, unit_rows, inverse, gain_row):
    scaled = grad_out * gain_row
    centred_grad = (
        scaled
        - jnp.mean(scaled, axis=-1, keepdims=True)
        - unit_rows * jnp.mean(scaled * unit_rows, axis=-1, keepdims=True)
    )
    return (
        centred_grad * inverse,
        jnp.sum(grad_out * unit_rows, axis=0),
        jnp.sum(grad_out, axis=0),
    )


def attend(packed, score_scale):
    query_rows = packed[:, 0]
    key_rows = packed[:, 1]
    value_rows = packed[:, 2]
    scores = contract_cols(query_rows, key_rows) * score_scale
    highest = jnp.max(scores, axis=-1, keepdims=True)
    powers = jnp.exp(scores - highest)
    totals = jnp.sum(powers, axis=-1, keepdims=True)
    softmax_rows = (powers / totals).astype(jnp.bfloat16)
    mixed_rows = jnp.dot(softmax_rows, value_rows, preferred_element_type=jnp.float32)
    return (mixed_rows.astype(jnp.bfloat16), highest[:, 0] + jnp.log(totals[:, 0]))


def attend_back(packed, grad_mixed, logsum, score_scale):
    query_rows = packed[:, 0]
    key_rows = packed[:, 1]
    value_rows = packed[:, 2]
    scores = contract_cols(query_rows, key_rows) * score_scale
    chances = jnp.exp(scores - logsum[:, None])
    grad_value = contract_rows(chances.astype(jnp.bfloat16), grad_mixed)
    grad_chances = contract_cols(grad_mixed, value_rows)
    offset = jnp.sum(grad_chances * chances, axis=-1, keepdims=True)
    grad_scores = (chances * (grad_chances - offset)).astype(jnp.bfloat16)
    grad_query = jnp.dot(grad_scores, key_rows, preferred_element_type=jnp.float32) * score_scale
    grad_key = contract_rows(grad_scores, query_rows) * score_scale
    return jnp.stack([grad_query, grad_key, grad_value], axis=1).astype(jnp.bfloat16)


def body(
    inputs,
    cotangent,
    time_table,
    timesteps,
    buckets,
    mixer_weight,
    output_weight,
    up_weight,
    down_weight,
    norm_gain,
    norm_shift,
    output_bias,
    up_bias,
):
    seq_count, tok_part, model_width = inputs.shape
    part_count = lax.axis_size("seq")
    seq_length = tok_part * part_count
    heads_here = HEADS // part_count
    row_count = seq_count * tok_part
    score_scale = 1.0 / math.sqrt(HEAD_SIZE)
    gains = norm_gain.astype(jnp.float32)
    shifts = norm_shift.astype(jnp.float32)
    biases = output_bias.astype(jnp.float32)
    up_vector = up_bias.astype(jnp.float32)
    embedded = jnp.take(time_table, timesteps, axis=0).astype(jnp.float32)
    summed_in = (inputs.astype(jnp.float32) + embedded[:, None, :]).reshape(row_count, model_width)
    normed_one, unit_one, inverse_one = normalize(summed_in, gains[0], shifts[0])
    low_one = normed_one.astype(jnp.bfloat16)
    projected = jnp.dot(low_one, mixer_weight, preferred_element_type=jnp.float32).astype(
        jnp.bfloat16
    )
    projected = projected.reshape(seq_count, tok_part, part_count, heads_here * 3 * HEAD_SIZE)
    block_in = lax.all_to_all(projected, "seq", split_axis=2, concat_axis=1, tiled=True)
    item_count = block_in.shape[0]
    stacked = block_in.reshape(item_count, seq_length, heads_here, 3, HEAD_SIZE).transpose(
        0, 2, 1, 3, 4
    )
    flat_items = stacked.reshape(item_count * heads_here, seq_length, 3, HEAD_SIZE)
    mixed_rows, logsum = lax.map(lambda single: attend(single, score_scale), flat_items)
    mixed_rows = mixed_rows.reshape(item_count, heads_here, seq_length, HEAD_SIZE).transpose(
        0, 2, 1, 3
    )
    mixed_heads, logsum, kept_heads = (
        mixed_rows.reshape(item_count, seq_length, 1, heads_here * HEAD_SIZE),
        logsum.reshape(item_count, heads_here, seq_length),
        stacked,
    )
    mixed_tokens = lax.all_to_all(
        mixed_heads, "seq", split_axis=1, concat_axis=2, tiled=True
    ).reshape(row_count, model_width)
    middle = (
        summed_in
        + jnp.dot(mixed_tokens, output_weight, preferred_element_type=jnp.float32)
        + biases[0]
    )
    normed_two, unit_two, inverse_two = normalize(middle, gains[1], shifts[1])
    low_two = normed_two.astype(jnp.bfloat16)
    raised = jnp.dot(low_two, up_weight, preferred_element_type=jnp.float32) + up_vector
    active, gelu_back = jax.vjp(exact_gelu, raised)
    hidden = active.astype(jnp.bfloat16)
    final_rows = (
        middle + jnp.dot(hidden, down_weight, preferred_element_type=jnp.float32) + biases[1]
    )
    layer_out = final_rows.astype(jnp.bfloat16).reshape(seq_count, tok_part, model_width)
    grad_low = cotangent.reshape(row_count, model_width)
    grad_final = grad_low.astype(jnp.float32)
    down_grad = contract_rows(hidden, grad_low)
    (grad_raised,) = gelu_back(contract_cols(grad_low, down_weight))
    raised_low = grad_raised.astype(jnp.bfloat16)
    up_grad = contract_rows(low_two, raised_low)
    grad_middle_norm, gain_two, shift_two = normalize_back(
        contract_cols(raised_low, up_weight), unit_two, inverse_two, gains[1]
    )
    grad_middle = grad_final + grad_middle_norm
    branch_low = grad_middle.astype(jnp.bfloat16)
    output_grad = contract_rows(mixed_tokens, branch_low)
    grad_mixed = contract_cols(branch_low, output_weight).astype(jnp.bfloat16)
    grad_mixed = grad_mixed.reshape(seq_count, tok_part, part_count, heads_here * HEAD_SIZE)
    grad_heads = lax.all_to_all(grad_mixed, "seq", split_axis=2, concat_axis=1, tiled=True)
    grad_items = grad_heads.reshape(seq_count, seq_length, heads_here, HEAD_SIZE).transpose(
        0, 2, 1, 3
    )
    grad_items = grad_items.reshape(seq_count * heads_here, seq_length, HEAD_SIZE)
    kept_items = kept_heads.reshape(seq_count * heads_here, seq_length, 3, HEAD_SIZE)
    logsum_items = logsum.reshape(seq_count * heads_here, seq_length)
    grad_packed = lax.map(
        lambda single: attend_back(single[0], single[1], single[2], score_scale),
        (kept_items, grad_items, logsum_items),
    )
    grad_packed = grad_packed.reshape(seq_count, heads_here, seq_length, 3 * HEAD_SIZE).transpose(
        0, 2, 1, 3
    )
    grad_packed = grad_packed.reshape(seq_count, seq_length, 1, heads_here * 3 * HEAD_SIZE)
    grad_projected = lax.all_to_all(
        grad_packed, "seq", split_axis=1, concat_axis=2, tiled=True
    ).reshape(row_count, 3 * model_width)
    mixer_grad = contract_rows(low_one, grad_projected)
    grad_start_norm, gain_one, shift_one = normalize_back(
        contract_cols(grad_projected, mixer_weight), unit_one, inverse_one, gains[0]
    )
    grad_start = grad_middle + grad_start_norm
    input_grad = grad_start.reshape(seq_count, tok_part, model_width)
    square_part = jnp.sum(
        (final_rows * final_rows).reshape(seq_count, tok_part * model_width), axis=1
    ) / (seq_length * model_width)
    bucket_hits = (buckets[:, None] == jnp.arange(BUCKETS, dtype=jnp.int32)[None, :]).astype(
        jnp.float32
    )
    gain_grad, shift_grad, bias_grad, up_bias_grad, bucket_norms, bucket_counts = lax.psum(
        (
            jnp.stack([gain_one, gain_two]),
            jnp.stack([shift_one, shift_two]),
            jnp.stack(
                [jnp.sum(branch_low.astype(jnp.float32), axis=0), jnp.sum(grad_final, axis=0)]
            ),
            jnp.sum(raised_low.astype(jnp.float32), axis=0),
            jnp.sum(bucket_hits * square_part[:, None], axis=0),
            jnp.sum(bucket_hits, axis=0) / part_count,
        ),
        ("dp", "seq"),
    )
    seq_sums = jnp.sum(input_grad, axis=1)
    step_values = timesteps.astype(jnp.float32)
    gathered_sums, gathered_steps = (
        lax.all_gather(seq_sums, ("dp", "seq"), axis=0, tiled=True),
        lax.all_gather(step_values, ("dp", "seq"), axis=0, tiled=True),
    )
    col_width = model_width // lax.axis_size("dp")
    col_start = lax.axis_index("dp") * col_width
    columns = lax.dynamic_slice_in_dim(gathered_sums, col_start, col_width, 1)
    step_hits = (gathered_steps[:, None] == jnp.arange(STEPS, dtype=jnp.float32)[None, :]).astype(
        jnp.float32
    )
    table_grad = lax.dot_general(
        step_hits,
        columns,
        (((0,), (0,)), ((), ())),
        precision=HIGH,
        preferred_element_type=jnp.float32,
    )
    share_mixer, share_output, share_up, share_down = (
        lax.psum_scatter(mixer_grad, "dp", scatter_dimension=0, tiled=True),
        lax.psum_scatter(output_grad, "dp", scatter_dimension=0, tiled=True),
        lax.psum_scatter(up_grad, "dp", scatter_dimension=0, tiled=True),
        lax.psum_scatter(down_grad, "dp", scatter_dimension=0, tiled=True),
    )
    final_mixer, final_output, final_up, final_down = (
        lax.psum(share_mixer.astype(jnp.bfloat16), "seq").astype(jnp.float32),
        lax.psum(share_output.astype(jnp.bfloat16), "seq").astype(jnp.float32),
        lax.psum(share_up.astype(jnp.bfloat16), "seq").astype(jnp.float32),
        lax.psum(share_down.astype(jnp.bfloat16), "seq").astype(jnp.float32),
    )
    return (
        layer_out,
        input_grad,
        final_mixer,
        final_output,
        final_up,
        final_down,
        gain_grad,
        shift_grad,
        bias_grad,
        up_bias_grad,
        table_grad,
        bucket_norms,
        bucket_counts,
    )


def solution(mesh):
    return jax.shard_map(
        body,
        mesh=mesh,
        in_specs=(
            P("dp", "seq", None),
            P("dp", "seq", None),
            P(),
            P("dp"),
            P("dp"),
            P(),
            P(),
            P(),
            P(),
            P(),
            P(),
            P(),
            P(),
        ),
        out_specs=(
            P("dp", "seq", None),
            P("dp", "seq", None),
            P("dp", None),
            P("dp", None),
            P("dp", None),
            P("dp", None),
            P(),
            P(),
            P(),
            P(),
            P(None, "dp"),
            P(),
            P(),
        ),
        check_vma=False,
    )
```

profile of v0, /device:TPU:0, one launch (start us, length us, event | category | flops | bytes accessed | tf_op | source)
XLA Modules:
  0.0 633.0 jit_solution(5926026508607208544)
XLA Ops:
  20.6 3.4 convolution_convert_fusion
  24.0 6.5 %reshape.285 = bf16[2,256,4,576]{3,2,1,0:T(4,128)(2,1)} reshape(bf16[512,2304]{1,0:T(8,128)(2,1)} %convolution_convert_fusion) | data formatting | bytes 4718592 | tf_op jit(solution)/shard_map/reshape | solution.py:117
  30.5 7.9 %copy.71 = bf16[2,256,4,576]{1,0,3,2:T(2,128)(2,1)} copy(bf16[2,256,4,576]{3,2,1,0:T(4,128)(2,1)} %reshape.285) | data formatting | bytes 4718592 | tf_op jit(solution)/shard_map/reshape | solution.py:117
  38.5 6.3 all-to-all-start
  44.8 53.9 %all-to-all-done = bf16[2,256,4,576]{1,0,3,2:T(2,128)(2,1)} async-done(((bf16[2,256,4,576]{1,0,3,2:T(2,128)(2,1)}), bf16[2,256,4,576]{1,0,3,2:T(2,128)(2,1)}, u32[]{:S(2)}, u32[]{:S(2)}) %all-to-all-start) | async-done | bytes 2359328 | tf_op jit(solution)/shard_map/all_to_all | solution.py:118
  98.7 4.9 copy.61
  103.6 5.4 reshape.258
  109.0 33.2 %while.22 = (s32[]{:T(128)}, bf16[6,1024,64]{1,2,0:T(8,128)(2,1)}, f32[6,1024]{1,0:T(8,128)}, bf16[6,1024,3,64]{1,3,2,0:T(8,128)(2,1)}, s32[]{:T(128)}, /*index=5*/s32[]{:T(128)}) while((s32[]{:T(128)}, bf16[6,1024,64]{1,2,0:T(8,128)(2,1)}, f32[6,1024]{1,0:T(8,128)}, bf16[6,1024,3,64]{1,3,2,0:T(8,128)(2,1)}, s32[]{:T(128)}, ...), condition=%wide.region_5.6_spmd, body=%wide.region_2.0_spmd.sunk | while | flops 277937152 | bytes 13934681 | solution.py:124
  142.2 3.6 copy.62
  145.8 4.2 all-to-all-start.1
  151.7 23.6 %all-to-all-done.1 = bf16[2,1024,1,192]{3,0,2,1:T(2,128)(2,1)} async-done(((bf16[2,1024,1,192]{3,0,2,1:T(2,128)(2,1)}), bf16[2,1024,1,192]{3,0,2,1:T(2,128)(2,1)}, u32[]{:S(2)}, u32[]{:S(2)}) %all-to-all-start.1) | async-done | bytes 786464 | tf_op jit(solution)/shard_map/all_to_all | solution.py:133
  175.4 3.8 copy.72
  182.8 5.3 fusion.49
  188.2 19.1 %convert_reduce_fusion = (f32[3072]{0:T(1024)}, bf16[512,3072]{1,0:T(8,128)(2,1)S(1)}, f32[512,3072]{1,0:T(8,128)}) fusion(f32[512,3072]{1,0:T(8,128)S(1)} %fusion.49, f32[3072]{0:T(1024)S(1)} %convert_element_type.122, bf16[512,768]{1,0:T(8,128)(2,1)S(1)} %bitcast.197, bf16[3072,768]{1,0:T(8,128)(2,1)S(1)} %bitcast.215), kind=kOutput, calls=%fused_computation.46 | convolution fusion | flops 2533880832 | bytes 21258240 | tf_op jit(solution)/shard_map/dot_general | solution.py:25
  207.3 3.6 multiply_reduce_fusion.3
  216.1 9.0 %fusion.48 = f32[768,3072]{1,0:T(8,128)} fusion(bf16[512,3072]{1,0:T(8,128)(2,1)} %copy-done.31, f32[512,768]{1,0:T(8,128)} %copy-done.7, f32[768]{0:T(1024)} %get-tuple-element.103, f32[768]{0:T(1024)} %get-tuple-element.159, f32[512]{0:T(512)} %copy-done.23, f32[512]{0:T(512)S(1)} %broadcast_multiply_fusion.4), kind=kOutput, calls=%fused_computation.126 | convolution fusion | flops 2417885184 | bytes 14166016 | tf_op jit(solution)/shard_map/dot_general | solution.py:19
  225.2 3.6 convolution_convert_fusion.1
  234.0 4.2 all-to-all-start.2
  238.2 6.3 multiply_convert_fusion.1
  246.1 5.1 fusion.53
  251.5 6.2 all-to-all-done.2
  262.9 56.8 %while.23 = (s32[]{:T(128)}, bf16[6,1024,3,64]{1,3,2,0:T(8,128)(2,1)}, bf16[6,1024,3,64]{1,3,2,0:T(8,128)(2,1)}, f32[6,1024]{1,0:T(8,128)}, bf16[6,1024,64]{1,2,0:T(8,128)(2,1)}, /*index=5*/s32[]{:T(128)}) while((s32[]{:T(128)}, bf16[6,1024,3,64]{1,3,2,0:T(8,128)(2,1)}, bf16[6,1024,3,64]{1,3,2,0:T(8,128)(2,1)}, f32[6,1024]{1,0:T(8,128)}, ...), condition=%wide.region_12.13_spmd, body=%wide.region_10.12_spmd.sunk | while | flops 685177856 | bytes 34369632 | solution.py:171
  319.7 7.5 %copy.68 = bf16[2,1024,1,576]{3,0,2,1:T(2,128)(2,1)} copy(bf16[2,1024,1,576]{1,3,0,2:T(8,128)(2,1)} %bitcast.199) | data formatting | bytes 4718592 | tf_op jit(solution)/shard_map/reshape | solution.py:178
  327.2 63.4 %all_to_all.60 = bf16[2,1024,1,576]{3,0,2,1:T(2,128)(2,1)} all-to-all(bf16[2,1024,1,576]{3,0,2,1:T(2,128)(2,1)} %copy.68), channel_id=1, replica_groups=mesh['dp'=8,'seq'=4] {'seq'}, dimensions={1} | all-to-all | bytes 4718592 | tf_op jit(solution)/shard_map/all_to_all | solution.py:179
  390.6 7.8 %copy.73 = bf16[2,4,256,1,576]{2,1,4,0,3:T(4,128)(2,1)} copy(bf16[2,4,256,1,576]{4,0,2,1,3:T(2,128)(2,1)} %bitcast.185) | data formatting | bytes 4718592 | tf_op jit(solution)/shard_map/all_to_all | solution.py:179
  398.4 4.1 copy.70
  404.4 4.9 fusion.52
  411.6 7.9 %multiply_reduce_fusion.2 = (f32[512]{0:T(512)}, bf16[512,768]{1,0:T(8,128)(2,1)}) fusion(f32[768]{0:T(1024)S(1)} %copy-done.24, f32[512,768]{1,0:T(8,128)} %copy-done.7, bf16[512,3072]{1,0:T(8,128)(2,1)} %copy-done.13, bf16[3072,768]{1,0:T(8,128)(2,1)} %param.25), kind=kOutput, calls=%fused_computation.67 | convolution fusion | flops 2417884672 | bytes 10228736 | tf_op jit(solution)/shard_map/dot_general | solution.py:147
  431.5 56.0 %reduce-scatter.5.cloned.1.call-done = f32[96,2304]{1,0:T(8,128)} async-done(((f32[768,2304]{1,0:T(8,128)}), f32[96,2304]{1,0:T(8,128)}) %reduce-scatter.5.cloned.1.call-update) | async-done | bytes 884752 | tf_op jit(solution)/shard_map/reduce_scatter | solution.py:227
  489.5 4.8 multiply_reduce_fusion.4
  497.3 77.2 %all-gather = f32[32,2,768]{2,1,0:T(2,128)} all-gather(f32[1,2,768]{2,1,0:T(2,128)S(1)} %bitcast.205), channel_id=1, replica_groups=mesh['dp'=8,'seq'=4] {'dp','seq'}, dimensions={0}, use_global_device_ids=true | all-gather | bytes 202752 | tf_op jit(solution)/shard_map/all_gather | solution.py:210
  578.8 38.2 %all-reduce.1 = (f32[2,768]{1,0:T(2,128)}, f32[2,768]{1,0:T(2,128)}, f32[2,768]{1,0:T(2,128)}, f32[3072]{0:T(1024)}, f32[64]{0:T(128)S(1)}, /*index=5*/f32[8]{0:T(128)}, f32[8]{0:T(128)}) all-reduce(f32[2,768]{1,0:T(2,128)} %pad_maximum_fusion, f32[2,768]{1,0:T(2,128)} %pad_maximum_fusion.1, ...), channel_id=1, replica_groups=mesh['dp'=8,'seq'=4] {'dp','seq'}, use_global_device_ids=true, to_apply=%region_25.26 | all-reduce | flops 7760 | bytes 62080 | tf_op jit(solution)/shard_map/psum | solution.py:194
  (246 shorter events, 160.3 us)
Async XLA Ops:
  7.2 13.4 %copy-start = (bf16[768,2304]{1,0:T(8,128)(2,1)S(1)}, bf16[768,2304]{1,0:T(8,128)(2,1)}, u32[]{:S(2)}) copy-start(bf16[768,2304]{1,0:T(8,128)(2,1)} %param.22) | copy-start | bytes 10616836
  13.1 6.0 copy-start.17
  14.7 4.4 copy-start.19
  16.7 2.4 copy-start.15
  38.5 60.2 %all-to-all-start = ((bf16[2,256,4,576]{1,0,3,2:T(2,128)(2,1)}), bf16[2,256,4,576]{1,0,3,2:T(2,128)(2,1)}, u32[]{:S(2)}, u32[]{:S(2)}) async-start(bf16[2,256,4,576]{1,0,3,2:T(2,128)(2,1)} %copy.71), calls=%async_computation | async-start | bytes 4718592 | tf_op jit(solution)/shard_map/all_to_all | solution.py:118
  142.2 8.2 %copy-start.27 = (bf16[2,768]{1,0:T(2,128)(2,1)S(1)}, bf16[2,768]{1,0:T(2,128)(2,1)}, u32[]{:S(2)}) copy-start(bf16[2,768]{1,0:T(2,128)(2,1)} %param.28) | copy-start | bytes 9220
  145.8 29.5 %all-to-all-start.1 = ((bf16[2,1024,1,192]{3,0,2,1:T(2,128)(2,1)}), bf16[2,1024,1,192]{3,0,2,1:T(2,128)(2,1)}, u32[]{:S(2)}, u32[]{:S(2)}) async-start(bf16[2,1024,1,192]{3,0,2,1:T(2,128)(2,1)} %copy.62), calls=%async_computation.1 | async-start | bytes 2097152 | tf_op jit(solution)/shard_map/all_to_all | solution.py:133
  150.1 275.0 %reduce-scatter.7.cloned.1.call-start = ((), (), s32[]{:S(2)}) async-start(), calls=%async_computation.9 | async-start | bytes 2654208 | tf_op jit(solution)/shard_map/reduce_scatter | solution.py:228
  179.2 2.3 copy-start.29
  181.5 6.7 %slice-start.2 = ((s8[4718592]{0:T(1024)(128)(4,1)}), s8[4194304]{0:T(1024)(128)(4,1)S(1)}, s32[]{:S(2)}) async-start(s8[4718592]{0:T(1024)(128)(4,1)} %bitcast.214), calls=%async_computation.15 | async-start | bytes 8388608
  182.4 28.4 %copy-start.7 = (f32[512,768]{1,0:T(8,128)}, f32[512,768]{1,0:T(8,128)S(1)}, u32[]{:S(2)}) copy-start(f32[512,768]{1,0:T(8,128)S(1)} %get-tuple-element.154) | copy-start | bytes 4718596
  182.7 28.1 %copy-start.23 = (f32[512]{0:T(512)}, f32[512]{0:T(512)S(1)}, u32[]{:S(2)}) copy-start(f32[512]{0:T(512)S(1)} %add_rsqrt_fusion) | copy-start | bytes 6148
  182.8 5.4 copy-start.11
  182.8 5.4 slice-start.3
  182.8 24.5 %slice-start = ((s8[4718592]{0:T(1024)(128)(4,1)}), s8[4194304]{0:T(1024)(128)(4,1)S(1)}, s32[]{:S(2)}) async-start(s8[4718592]{0:T(1024)(128)(4,1)} %bitcast.212), calls=%async_computation.13 | async-start | bytes 8388608
  188.1 19.1 %copy-start.9 = (f32[512,3072]{1,0:T(8,128)}, f32[512,3072]{1,0:T(8,128)S(1)}, u32[]{:S(2)}) copy-start(f32[512,3072]{1,0:T(8,128)S(1)} %fusion.49) | copy-start | bytes 18874372
  188.2 19.1 %slice-start.1 = ((s8[4718592]{0:T(1024)(128)(4,1)}), s8[524288]{0:T(1024)(128)(4,1)S(1)}, s32[]{:S(2)}) async-start(s8[4718592]{0:T(1024)(128)(4,1)} %bitcast.212), calls=%async_computation.14 | async-start | bytes 1048576
  207.3 3.6 copy-start.31
  215.5 211.2 %reduce-scatter.9.cloned.1.call-start = ((), (), s32[]{:S(2)}) async-start(), calls=%async_computation.10 | async-start | bytes 10616832 | tf_op jit(solution)/shard_map/reduce_scatter | solution.py:229
  234.0 23.8 %all-to-all-start.2 = ((bf16[2,256,4,192]{1,0,3,2:T(2,128)(2,1)}), bf16[2,256,4,192]{1,0,3,2:T(2,128)(2,1)}, u32[]{:S(2)}, u32[]{:S(2)}) async-start(bf16[2,256,4,192]{1,0,3,2:T(2,128)(2,1)} %reshape.265), calls=%async_computation.2 | async-start | bytes 1572864 | tf_op jit(solution)/shard_map/all_to_all | solution.py:164
  238.2 190.9 %reduce-scatter.11.cloned.1.call-start = ((), (), s32[]{:S(2)}) async-start(), calls=%async_computation.11 | async-start | bytes 10616832 | tf_op jit(solution)/shard_map/reduce_scatter | solution.py:230
  238.2 7.9 %copy-start.12 = (bf16[2,256,768]{2,1,0:T(8,128)(2,1)S(1)}, bf16[2,256,768]{2,1,0:T(8,128)(2,1)}, u32[]{:S(2)}) copy-start(bf16[2,256,768]{2,1,0:T(8,128)(2,1)} %param.18) | copy-start | bytes 2359300
  251.3 236.2 %reduce-scatter.5.cloned.1.call-start = ((), (), s32[]{:S(2)}) async-start(), calls=%async_computation.8 | async-start | bytes 7962624 | tf_op jit(solution)/shard_map/reduce_scatter | solution.py:227
  409.4 210.0 %all-reduce.5.cloned.1.call-start = ((), (), s32[]{:S(2)}) async-start(), calls=%async_computation.12 | async-start | bytes 3538944 | tf_op jit(solution)/shard_map/psum | solution.py:233
  411.6 10.5 %copy-start.22 = (f32[768]{0:T(1024)S(1)}, f32[768]{0:T(1024)}, u32[]{:S(2)}) copy-start(f32[768]{0:T(1024)} %get-tuple-element.139) | copy-start | bytes 9220
  411.6 10.5 %copy-start.26 = (f32[768]{0:T(1024)S(1)}, f32[768]{0:T(1024)}, u32[]{:S(2)}) copy-start(f32[768]{0:T(1024)} %get-tuple-element.98) | copy-start | bytes 9220
  426.7 62.7 %copy-start.16 = (f32[768]{0:T(1024)S(1)}, f32[768]{0:T(1024)}, u32[]{:S(2)}) copy-start(f32[768]{0:T(1024)} %copy-done.15) | copy-start | bytes 9220
  426.7 62.7 %copy-start.18 = (f32[1,2,2,128]{3,1,2,0:T(2,128)S(1)}, f32[1,2,2,128]{3,1,2,0:T(2,128)}, u32[]{:S(2)}) copy-start(f32[1,2,2,128]{3,1,2,0:T(2,128)} %copy-done.17) | copy-start | bytes 6148
  489.5 6.0 copy-start.3
  489.5 6.0 copy-start.5
  489.5 6.0 copy-start.20
  619.3 5.9 copy-start.14
  (12 other events, 17.3 us)
Sparse Core Ops, SparseCore 0:
  215.6 41.5 reduce-scatter.6
  261.1 76.5 reduce-scatter.8
  341.6 76.4 reduce-scatter.10
  421.9 65.4 reduce-scatter.4
  490.5 79.9 all-reduce.4
where the time goes:
time: 645 us; the launch traced here: 633 us
  blocking collectives  179 us (28%)
  waiting for transfers between devices  140 us (22%)
  matrix products  121 us (19%)
  local copies, waits for them, and re-layouts  107 us (17%)
  other arithmetic  56.5 us (9%)
  starting transfers between devices  15.9 us (2%)
  between operations  14.5 us (2%)
    all_gather x1, blocking collectives, body(): lax.all_gather(seq_sums, ('dp', 'seq'), axis=0, tiled=True)  77.2 us
    all_to_all x1, blocking collectives, body(): lax.all_to_all(grad_packed, 'seq', split_axis=1, concat_axis=2, tiled=True)  63.4 us
    reduce_scatter x1, waiting for transfers between devices, body(): lax.psum_scatter(mixer_grad, 'dp', scatter_dimension=0, tiled=True)  56 us
    all_to_all x1, waiting for transfers between devices, body(): lax.all_to_all(projected, 'seq', split_axis=2, concat_axis=1, tiled=True)  53.9 us
    dot_general x22, matrix products, contract_cols(): lax.dot_general(left_side, right_side, (((1,), (1,)), ((), ())), preferre...  51.7 us
    psum x1, blocking collectives, body(): lax.psum((jnp.stack([gain_one, gain_two]), jnp.stack([shift_one, shift_tw...  38.2 us
    dot_general x16, matrix products, contract_rows(): lax.dot_general(left_side, right_side, (((0,), (0,)), ((), ())), preferre...  36.5 us
    all_to_all x1, waiting for transfers between devices, body(): lax.all_to_all(mixed_heads, 'seq', split_axis=1, concat_axis=2, tiled=True)  23.6 us
  transfers between devices with their start and end apart: 8, of which 4 were waited for; matrix products, arithmetic and copies ran while one was open for 24% of the time, Pallas kernels for 0%

commit v1 on v0

v1 whole, which is shorter than its diff:
```python
import functools
import math

import jax
import jax.numpy as jnp
from jax import lax
from jax.experimental import pallas as pl
from jax.experimental.pallas import tpu as pltpu
from jax.sharding import PartitionSpec as P

HEADS = 12
HEAD_SIZE = 64
PAIRS = HEADS // 2
PAIR = 2 * HEAD_SIZE
STEPS = 2000
BUCKETS = 8
EPS = 1e-05

BF = jnp.bfloat16
F32 = jnp.float32
MESH = pl.DeviceIdType.MESH


def mm(a, b):
    return lax.dot_general(a, b, (((1,), (0,)), ((), ())), preferred_element_type=F32)


def mm_nt(a, b):
    return lax.dot_general(a, b, (((1,), (1,)), ((), ())), preferred_element_type=F32)


def mm_tn(a, b):
    return lax.dot_general(a, b, (((0,), (0,)), ((), ())), preferred_element_type=F32)


def iota(shape, axis):
    return lax.broadcasted_iota(jnp.int32, shape, axis)


def place():
    d, z = lax.axis_index("dp"), lax.axis_index("seq")
    return d, z, lax.rem(d, 2), lax.div(d, 2)


def column_peers():
    d, z, c, k = place()
    found = []
    for off in range(1, 8):
        m = lax.rem(c * 4 + z + off, 8)
        found.append((2 * k + lax.div(m, 4), lax.rem(m, 4)))
    return found


def greet(ids):
    barrier = pltpu.get_barrier_semaphore()
    for one in ids:
        pl.semaphore_signal(barrier, inc=1, device_id=one, device_id_type=MESH)
    pl.semaphore_wait(barrier, len(ids))


def swap_part(i):
    d, z, c, k = place()
    core, chip = lax.div(z, 2), 2 * c + i
    return core, chip, jnp.logical_and(core == c, chip == z), 2 * k + core


def swap_start(source, target, send, recv):
    z = lax.axis_index("seq")
    slot = lax.rem(z, 2)
    for i in range(2):
        core, chip, own, there = swap_part(i)

        @pl.when(own)
        def _():
            pltpu.make_async_copy(source(i), target(slot), recv.at[slot]).start()

        @pl.when(jnp.logical_not(own))
        def _():
            pltpu.make_async_remote_copy(
                source(i), target(slot), send.at[i], recv.at[slot],
                device_id=(there, chip), device_id_type=MESH,
            ).start()


def swap_wait(target, recv, s):
    pltpu.make_async_copy(target(s), target(s), recv.at[s]).wait()


def swap_sent(source, target, send, recv):
    for i in range(2):
        core, chip, own, there = swap_part(i)

        @pl.when(jnp.logical_not(own))
        def _():
            pltpu.make_async_remote_copy(
                source(i), target(i), send.at[i], recv.at[i],
                device_id=(there, chip), device_id_type=MESH,
            ).wait_send()


def forward_kernel(
    ts, x, cot, table, wm, wo, wu, wd, gains, shifts, biases, upb,
    lout, s_out, low1_out, q_out, kv_out, ls_out, do_out, dt_out, gm_out, g_out, small_out,
    xr, cr, embs, embr, tabv, wmv, wov, wuv, wdv, sv, low1, q2, kv, mixed, ls, lst,
    mid, low2, low2t, hid, rl, gf, lov, dov, dtv, gmv, gv, small, upg, sqv,
    xsend, xrecv, csend, crecv, esend, erecv, ksend, krecv, wsem, osem,
):
    d, z, c, k = place()
    toks, width = xr.shape
    part = toks // 2
    hidden_width = wuv.shape[1]

    def fetch(i, src, dst):
        return pltpu.make_async_copy(src, dst, wsem.at[i])

    def put(i, src, dst):
        return pltpu.make_async_copy(src, dst, osem.at[i])

    fetch(0, table, tabv).start()
    greet(column_peers())
    x_at = lambda s: xr.at[pl.ds(pl.multiple_of(s * part, part), part)]
    c_at = lambda s: cr.at[pl.ds(pl.multiple_of(s * part, part), part)]
    swap_start(lambda i: x.at[i], x_at, xsend, xrecv)
    fetch(1, wm, wmv).start()
    fetch(2, wo, wov).start()
    fetch(3, wu, wuv).start()
    fetch(4, wd, wdv).start()
    fetch(0, table, tabv).wait()
    row, col = iota((16, tabv.shape[0]), 0), iota((16, tabv.shape[0]), 1)
    wanted = jnp.where(row == 0, ts[0], ts[1])
    picked = mm(jnp.where(jnp.logical_and(col == wanted, row < 2), 1.0, 0.0).astype(BF), tabv[...])
    for i in range(2):
        embs[i] = jnp.broadcast_to(picked[i : i + 1], (16, width)).astype(BF)
    swap_start(lambda i: embs.at[i], lambda s: embr.at[s], esend, erecv)
    for s in range(2):
        swap_wait(lambda s: embr.at[s], erecv, s)
    for s in range(2):
        swap_wait(x_at, xrecv, s)
    swap_start(lambda i: cot.at[i], c_at, csend, crecv)
    gain0, shift0 = gains[0:1, :].astype(F32), shifts[0:1, :].astype(F32)
    gain1, shift1 = gains[1:2, :].astype(F32), shifts[1:2, :].astype(F32)
    bias0, bias1 = biases[0:1, :].astype(F32), biases[1:2, :].astype(F32)

    for s in range(2):
        emb = embr[s][0:1, :].astype(F32)

        @pl.loop(0, part // 128)
        def _(b):
            rows = pl.ds(pl.multiple_of(s * part + b * 128, 128), 128)
            v = xr[rows, :].astype(F32) + emb
            cen = v - jnp.mean(v, axis=-1, keepdims=True)
            inv = lax.rsqrt(jnp.mean(cen * cen, axis=-1, keepdims=True) + EPS)
            sv[rows, :] = v
            low1[rows, :] = (cen * inv * gain0 + shift0).astype(BF)

    put(0, sv, s_out).start()
    put(1, low1, low1_out).start()

    mine = pl.ds(pl.multiple_of(c * toks, toks), toks)
    partner = d + 1 - 2 * c

    def kv_copy(p):
        return pltpu.make_async_remote_copy(
            kv.at[p, :, mine], kv.at[p, :, mine], ksend.at[p], krecv.at[p],
            device_id=(partner, z), device_id_type=MESH,
        )

    fetch(1, wm, wmv).wait()
    low_half = iota((1, PAIR), 1) < HEAD_SIZE

    @pl.loop(0, PAIRS)
    def _(p):
        cols = pl.ds(pl.multiple_of(p * 3 * PAIR, PAIR), 3 * PAIR)
        res = mm(low1[...], wmv[:, cols])
        t0, t1, t2 = res[:, :PAIR], res[:, PAIR : 2 * PAIR], res[:, 2 * PAIR :]
        q2[p] = (jnp.where(low_half, t0, t1).astype(BF) * 0.125).astype(BF)
        kv[p, 0, mine, :] = pltpu.roll(jnp.where(low_half, t2, t0), HEAD_SIZE, 1).astype(BF)
        kv[p, 1, mine, :] = jnp.where(low_half, t1, t2).astype(BF)
        kv_copy(p).start()

    put(2, q2, q_out).start()

    lane = iota((1, PAIR), 1)
    blk = toks // 2

    @pl.loop(0, PAIRS)
    def _(p):
        kv_copy(p).wait_recv()

        @pl.loop(0, 2)
        def _(b):
            rows = pl.ds(pl.multiple_of(b * blk, blk), blk)
            q = q2[p, rows, :]
            keys, vals = kv[p, 0], kv[p, 1]
            outs, sums = [], []
            for h in range(2):
                own = low_half if h == 0 else jnp.logical_not(low_half)
                s = mm_nt(jnp.where(own, q, jnp.zeros_like(q)), keys)
                top = jnp.max(s, axis=-1, keepdims=True)
                e = jnp.exp(s - top)
                total = jnp.sum(e, axis=-1, keepdims=True)
                outs.append(mm(e.astype(BF), vals) * (1.0 / total))
                sums.append(top + jnp.log(total))
            cols = pl.ds(pl.multiple_of(p * PAIR, PAIR), PAIR)
            mixed[rows, cols] = jnp.where(low_half, outs[0], outs[1]).astype(BF)
            ls[rows, :] = jnp.where(
                lane == 2 * p, sums[0], jnp.where(lane == 2 * p + 1, sums[1], ls[rows, :])
            )

    put(3, kv, kv_out).start()
    lst[...] = ls[...].T
    put(4, lst, ls_out).start()
    fetch(2, wo, wov).wait()

    @pl.loop(0, 2)
    def _(b):
        rows = pl.ds(pl.multiple_of(b * blk, blk), blk)
        v = sv[rows, :] + mm(mixed[rows, :], wov[...]) + bias0
        mid[rows, :] = v
        cen = v - jnp.mean(v, axis=-1, keepdims=True)
        inv = lax.rsqrt(jnp.mean(cen * cen, axis=-1, keepdims=True) + EPS)
        low = cen * inv * gain1 + shift1
        low2[rows, :] = low.astype(BF)

    low2t[...] = low2[...].T
    fetch(3, wu, wuv).wait()
    fetch(4, wd, wdv).wait()
    for s in range(2):
        swap_wait(c_at, crecv, s)
    step = 256

    @pl.loop(0, hidden_width // step)
    def _(j):
        cols = pl.ds(pl.multiple_of(j * step, step), step)
        r = mm(low2[...], wuv[:, cols]) + upb[:, cols].astype(F32)
        back = mm_nt(cr[...], wdv[cols, :])
        half = 0.5 * (1.0 + lax.erf(r * math.sqrt(0.5)))
        bell = jnp.exp(r * r * -0.5) * (1.0 / math.sqrt(2.0 * math.pi))
        hid[:, cols] = (r * half).astype(BF)
        low = (back * (half + r * bell)).astype(BF)
        rl[:, cols] = low
        upg[:, cols] = jnp.sum(low.astype(F32), axis=0, keepdims=True)

    @pl.loop(0, width // step)
    def _(j):
        cols = pl.ds(pl.multiple_of(j * step, step), step)
        fin = mid[:, cols] + mm(hid[...], wdv[:, cols]) + biases[1:2, cols].astype(F32)
        lov[:, cols] = fin.astype(BF)
        sqv[:, cols] = jnp.sum(fin * fin, axis=0, keepdims=True)
        gf[:, cols] = mm_nt(rl[...], wuv[cols, :])

    put(5, lov, lout).start()
    shard = hidden_width // 8
    quarter = shard // 4

    def slot(s):
        return lax.div(s, 4), lax.rem(lax.div(s, 2), 2), lax.rem(s, 2)

    @pl.loop(0, 8)
    def _(s):
        cols = pl.ds(pl.multiple_of(s * shard, shard), shard)
        res = mm_tn(hid[:, cols], cr[...]).astype(BF)
        b2, b1, b0 = slot(s)
        for i in range(4):
            gv[i, b2, b1, b0] = res[i * quarter : (i + 1) * quarter]

    @pl.loop(0, 4)
    def _(j):
        cols = pl.ds(pl.multiple_of(j * width, width), width)
        for h in range(2):
            res = mm(low2t[h * width // 2 : (h + 1) * width // 2, :], rl[:, cols]).astype(BF)
            for i in range(4):
                gv[4 + j, h, i // 2, i % 2] = res[i * quarter : (i + 1) * quarter]

    small[...] = jnp.zeros_like(small)

    @pl.loop(0, toks // 128)
    def _(b):
        rows = pl.ds(pl.multiple_of(b * 128, 128), 128)
        v = mid[rows, :]
        cen = v - jnp.mean(v, axis=-1, keepdims=True)
        inv = lax.rsqrt(jnp.mean(cen * cen, axis=-1, keepdims=True) + EPS)
        unit = cen * inv
        raw = gf[rows, :]
        g = raw * gain1
        centred = (
            g - jnp.mean(g, axis=-1, keepdims=True)
            - unit * jnp.mean(g * unit, axis=-1, keepdims=True)
        )
        ct = cr[rows, :].astype(F32)
        grad = ct + centred * inv
        low = grad.astype(BF)
        gmv[rows, :] = grad
        small[0:1, :] += jnp.sum(raw * unit, axis=0, keepdims=True)
        small[1:2, :] += jnp.sum(raw, axis=0, keepdims=True)
        small[2:3, :] += jnp.sum(low.astype(F32), axis=0, keepdims=True)
        small[3:4, :] += jnp.sum(ct, axis=0, keepdims=True)

    put(6, gmv, gm_out).start()
    for i in range(4):
        small[4 + i : 5 + i, :] = upg[:, i * width : (i + 1) * width]
    small[8:9, :] = sqv[...]

    fold = jnp.where(lax.div(iota((PAIR, width), 1), HEAD_SIZE) == iota((PAIR, width), 0), 1.0, 0.0)
    fold = fold.astype(BF)

    @pl.loop(0, 2)
    def _(b):
        rows = pl.ds(pl.multiple_of(b * blk, blk), blk)
        dout = mm_nt(gmv[rows, :].astype(BF), wov[...]).astype(BF)
        dov[rows, :] = dout
        prod = dout.astype(F32) * mixed[rows, :].astype(F32)
        high = prod.astype(BF)
        rest = (prod - high.astype(F32)).astype(BF)
        dtv[:, rows] = mm_nt(fold, high) + mm_nt(fold, rest)

    put(7, dov, do_out).start()
    put(8, dtv, dt_out).start()
    for h in range(2):
        res = mm_tn(mixed[:, h * width // 2 : (h + 1) * width // 2], gmv[...].astype(BF)).astype(BF)
        for i in range(4):
            gv[8, h, i // 2, i % 2] = res[i * quarter : (i + 1) * quarter]
    put(9, gv, g_out).start()
    put(10, small, small_out).start()

    swap_sent(lambda i: x.at[i], x_at, xsend, xrecv)
    swap_sent(lambda i: cot.at[i], c_at, csend, crecv)
    swap_sent(lambda i: embs.at[i], lambda s: embr.at[s], esend, erecv)

    @pl.loop(0, PAIRS)
    def _(p):
        kv_copy(p).wait_send()

    for i, (src, dst) in enumerate((
        (sv, s_out), (low1, low1_out), (q2, q_out), (kv, kv_out), (lst, ls_out), (lov, lout),
        (gmv, gm_out), (dov, do_out), (dtv, dt_out), (gv, g_out), (small, small_out),
    )):
        put(i, src, dst).wait()


def sds(shape, dtype):
    return jax.ShapeDtypeStruct(shape, dtype)


def run_forward(ts, x, cot, table, wm, wo, wu, wd, gains, shifts, biases, upb):
    seqs, part, width = x.shape
    toks = 2 * part
    ff = wu.shape[1]
    shard = width // 8
    outs = dict(
        lout=sds((toks, width), BF), s=sds((toks, width), F32), low1=sds((toks, width), BF),
        q=sds((PAIRS, toks, PAIR), BF), kv=sds((PAIRS, 2, 2 * toks, PAIR), BF),
        ls=sds((PAIR, toks), F32), do=sds((toks, width), BF), dt=sds((PAIR, toks), F32),
        gm=sds((toks, width), F32), g=sds((9, 2, 2, 2, shard, width), BF), small=sds((16, width), F32),
    )
    vm = lambda shape, dtype: pltpu.VMEM(shape, dtype)
    any_ = pl.BlockSpec(memory_space=pl.ANY)
    vmem = pl.BlockSpec(memory_space=pltpu.VMEM)
    dma = lambda *n: pltpu.SemaphoreType.DMA(n)
    res = pl.pallas_call(
        forward_kernel,
        out_shape=tuple(outs.values()),
        in_specs=[pl.BlockSpec(memory_space=pltpu.SMEM)] + [any_] * 7 + [vmem] * 4,
        out_specs=tuple([any_] * len(outs)),
        scratch_shapes=[
            vm((toks, width), BF), vm((toks, width), BF), vm((2, 16, width), BF), vm((2, 16, width), BF),
            vm(table.shape, BF), vm(wm.shape, BF), vm(wo.shape, BF), vm(wu.shape, BF), vm(wd.shape, BF),
            vm((toks, width), F32), vm((toks, width), BF), vm((PAIRS, toks, PAIR), BF),
            vm((PAIRS, 2, 2 * toks, PAIR), BF), vm((toks, width), BF), vm((toks, PAIR), F32),
            vm((PAIR, toks), F32), vm((toks, width), F32), vm((toks, width), BF), vm((width, toks), BF),
            vm((toks, ff), BF), vm((toks, ff), BF), vm((toks, width), F32), vm((toks, width), BF),
            vm((toks, width), BF), vm((PAIR, toks), F32), vm((toks, width), F32),
            vm((9, 2, 2, 2, shard, width), BF), vm((16, width), F32), vm((1, ff), F32), vm((1, width), F32),
            dma(2), dma(2), dma(2), dma(2), dma(2), dma(2), dma(PAIRS), dma(PAIRS), dma(5), dma(11),
        ],
        compiler_params=pltpu.CompilerParams(
            collective_id=0, has_side_effects=True, vmem_limit_bytes=60 << 20
        ),
        cost_estimate=pl.CostEstimate(flops=16_000_000_000, bytes_accessed=50_000_000, transcendentals=10_000_000),
        name="forward",
    )(ts, x, cot, table, wm, wo, wu, wd, gains, shifts, biases, upb.reshape(1, ff))
    return dict(zip(outs, res))


def flip(index, bit):
    return index + bit - 2 * bit * lax.rem(lax.div(index, bit), 2)


def bit_of(index, bit):
    return lax.rem(lax.div(index, bit), 2)


def axis_bits(size):
    found, bit = [], 1
    while bit < size:
        found.append(bit)
        bit *= 2
    return found


def add_into(dst, src):
    dst[...] = (dst[...].astype(F32) + src[...].astype(F32)).astype(dst.dtype)


class Reduction:
    STAGES = 7

    def __init__(self, index, first, count, kind, refs, outer):
        self.index, self.first, self.count, self.kind = index, first, count, kind
        self.g, self.r0, self.r1, self.r2, self.r3, self.r4, self.f, self.send, self.recv = refs
        d, z, _, _ = place()
        self.b0, self.b1, self.b2 = bit_of(d, outer), bit_of(d, 2 * outer), bit_of(d, 4 * outer)
        self.p0 = (flip(d, outer), z)
        self.p1 = (flip(d, 2 * outer), z)
        self.p2 = (flip(d, 4 * outer), z)
        self.z0, self.z1 = lax.rem(z, 2), lax.div(z, 2)
        self.q0, self.q1 = (d, flip(z, 1)), (d, flip(z, 2))
        rows, cols = self.g.shape[-2] // 2, self.g.shape[-1] // 2
        at = lambda b, n: pl.ds(pl.multiple_of(b * n, n), n)
        self.rows, self.other_rows = at(self.z0, rows), at(1 - self.z0, rows)
        self.cols, self.other_cols = at(self.z1, cols), at(1 - self.z1, cols)
        self.stage = 0

    def copy(self, stage):
        u = pl.ds(self.first, self.count)
        b0, b1, b2 = self.b0, self.b1, self.b2
        if stage == 0:
            src, dst, to = self.g.at[u, :, :, 1 - b0], self.r0.at[u], self.p0
        elif stage == 1 and self.kind == "a":
            src, dst, to = self.g.at[u, :, 1 - b1, b0], self.r1.at[u], self.p1
        elif stage == 1:
            src, dst, to = self.g.at[u, 1 - b2, :, b0], self.r1.at[u], self.p2
        elif stage == 2 and self.kind == "a":
            src, dst, to = self.g.at[u, 1 - b2, b1, b0], self.r2.at[u], self.p2
        elif stage == 2:
            src, dst, to = self.g.at[u, b2, 1 - b1, b0], self.r2.at[u], self.p1
        elif stage == 3:
            src, dst, to = self.g.at[u, b2, b1, b0, self.other_rows], self.r3.at[u], self.q0
        elif stage == 4:
            src, dst, to = self.g.at[u, b2, b1, b0, self.rows, self.other_cols], self.r4.at[u], self.q1
        elif stage == 5:
            src = dst = self.f.at[u, self.rows, self.cols]
            to = self.q1
        else:
            src = dst = self.f.at[u, self.rows]
            to = self.q0
        return pltpu.make_async_remote_copy(
            src, dst, self.send.at[self.index, stage], self.recv.at[self.index, stage],
            device_id=to, device_id_type=MESH,
        )

    def start(self):
        self.copy(0).start()

    def take(self):
        stage = self.stage
        b0, b1, b2 = self.b0, self.b1, self.b2
        self.landed(stage)
        if stage == 0:

            @pl.loop(0, self.count * 4)
            def _(i):
                u, y, x = self.first + lax.div(i, 4), lax.rem(lax.div(i, 2), 2), lax.rem(i, 2)
                add_into(self.g.at[u, y, x, b0], self.r0.at[u, y, x])

        elif stage == 1:

            @pl.loop(0, self.count * 2)
            def _(i):
                u, j = self.first + lax.div(i, 2), lax.rem(i, 2)
                dst = self.g.at[u, j, b1, b0] if self.kind == "a" else self.g.at[u, b2, j, b0]
                add_into(dst, self.r1.at[u, j])

        elif stage <= 4:

            @pl.loop(0, self.count)
            def _(i):
                u = self.first + i
                own = self.g.at[u, b2, b1, b0]
                if stage == 2:
                    add_into(own, self.r2.at[u])
                elif stage == 3:
                    add_into(own.at[self.rows], self.r3.at[u])
                else:
                    mine = own.at[self.rows, self.cols][...].astype(F32)
                    self.f.at[u, self.rows, self.cols][...] = (mine + self.r4[u].astype(F32)).astype(BF)

        self.stage += 1
        if self.stage < self.STAGES:
            self.copy(self.stage).start()

    def landed(self, stage):
        if stage < 5:
            self.copy(stage).wait_recv()
            return
        u = pl.ds(self.first, self.count)
        if stage == 5:
            dst = self.f.at[u, self.rows, self.other_cols]
        else:
            dst = self.f.at[u, self.other_rows]
        pltpu.make_async_copy(dst, dst, self.recv.at[self.index, stage]).wait()

    def close(self):
        for stage in range(self.STAGES):
            self.copy(stage).wait_send()


GROUPS = ((0, 2, "a"), (2, 2, "a"), (4, 2, "b"), (6, 2, "b"), (8, 1, "a"), (9, 1, "b"), (10, 1, "a"), (11, 1, "b"))
UNITS = 12
PLAN = ((0, 2), (1, 3, 4), (0, 2), (1, 3, 4, 0, 2), (5, 0, 2), (1, 3, 4, 0, 2))
HEAD_ROWS = 16


def backward_kernel(
    bits, part_shape,
    ts, buckets, lout, s_in, low1_in, q_in, kv_in, ls_in, do_in, dt_in, gm_in, g_in, wm, small, gains,
    lhome, ihome, f_out, total_out,
    sv, low1, low1t, q2, kv, ls, do, dt, gm, wmv, dkvs, dkvr, dqa, own, dqkv, igv,
    g, r0, r1, r2, r3, r4, f, sm, sr,
    lsend, lrecv, isend, irecv, ksend, krecv, rsend, rrecv, ssend, srecv, wsem, osem,
):
    d, z, c, k = place()
    toks, width = sv.shape
    part = toks // 2
    outer = (1 << len(bits)) // 8
    load = lambda i, src, dst: pltpu.make_async_copy(src, dst, wsem.at[i])
    loads = (
        (g_in, g.at[pl.ds(0, 9)]), (q_in, q2), (kv_in, kv), (do_in, do), (ls_in, ls), (dt_in, dt),
        (low1_in, low1), (wm, wmv), (s_in, sv), (gm_in, gm),
    )
    for i, (src, dst) in enumerate(loads):
        load(i, src, dst).start()
    peers = column_peers() + [(flip(d, bit), z) for bit in bits if bit > 1]
    greet(peers)
    partner = flip(d, 1)
    l_at = lambda i: lout.at[pl.ds(i * part, part)]
    i_at = lambda i: igv.at[pl.ds(i * part, part)]
    swap_start(l_at, lambda s: lhome.at[s], lsend, lrecv)

    refs = (g, r0, r1, r2, r3, r4, f, rsend, rrecv)
    groups = [Reduction(i, *spec, refs, outer) for i, spec in enumerate(GROUPS)]
    load(0, *loads[0]).wait()
    for one in groups[:5]:
        one.start()
    for i in range(1, 7):
        load(i, *loads[i]).wait()
    low1t[...] = low1[...].T

    low_half = iota((1, PAIR), 1) < HEAD_SIZE
    high_half = jnp.logical_not(low_half)
    blk = 256

    def dkv_copy(p):
        return pltpu.make_async_remote_copy(
            dkvs.at[p], dkvr.at[p], ksend.at[p], krecv.at[p], device_id=(partner, z), device_id_type=MESH
        )

    def attend(p, base, store):
        @pl.loop(0, toks // blk)
        def _(b):
            rows = pl.ds(pl.multiple_of(base + b * blk, blk), blk)
            keys, vals = kv[p, 0, rows, :], kv[p, 1, rows, :]
            cols = pl.ds(pl.multiple_of(p * PAIR, PAIR), PAIR)
            q, dout = q2[p], do[:, cols]
            dks, dvs, dq = [], [], None
            for h in range(2):
                half = low_half if h == 0 else high_half
                kh = jnp.where(half, keys, jnp.zeros_like(keys))
                vh = jnp.where(half, vals, jnp.zeros_like(vals))
                probs = jnp.exp(mm_nt(kh, q) - ls[pl.ds(2 * p + h, 1), :])
                ds = (probs * (mm_nt(vh, dout) - dt[pl.ds(2 * p + h, 1), :])).astype(BF)
                dvs.append(mm(probs.astype(BF), dout))
                dks.append(mm(ds, q))
                one = mm_tn(ds, kh)
                dq = one if dq is None else dq + one
            dqa[...] += dq
            store(pl.ds(pl.multiple_of(b * blk, blk), blk),
                  jnp.where(low_half, dks[0], dks[1]), jnp.where(low_half, dvs[0], dvs[1]))

    @pl.loop(0, PAIRS)
    def _(p):
        dqa[...] = jnp.zeros_like(dqa)

        def store_other(rows, dk, dv):
            dkvs[p, 0, rows, :] = dk.astype(BF)
            dkvs[p, 1, rows, :] = dv.astype(BF)

        def store_own(rows, dk, dv):
            own[0, rows, :] = dk
            own[1, rows, :] = dv

        attend(p, (1 - c) * toks, store_other)
        dkv_copy(p).start()
        attend(p, c * toks, store_own)
        dkv_copy(p).wait_recv()
        dq = dqa[...] * 0.125
        dk = pltpu.roll(own[0] + dkvr[p, 0].astype(F32), HEAD_SIZE, 1)
        dv = own[1] + dkvr[p, 1].astype(F32)
        first = pl.multiple_of(p * 3 * PAIR, PAIR)
        dqkv[:, pl.ds(first, PAIR)] = jnp.where(low_half, dq, dk).astype(BF)
        dqkv[:, pl.ds(first + PAIR, PAIR)] = jnp.where(low_half, dv, dq).astype(BF)
        dqkv[:, pl.ds(first + 2 * PAIR, PAIR)] = jnp.where(low_half, dk, dv).astype(BF)

        for i in range(PAIRS):

            @pl.when(p == i)
            def _():
                for one in PLAN[i]:
                    groups[one].take()
                if i % 2 == 1:
                    b = i // 2
                    for h in range(2):
                        res = mm(
                            low1t[h * width // 2 : (h + 1) * width // 2, :],
                            dqkv[:, b * width : (b + 1) * width],
                        ).astype(BF)
                        n = g.shape[-2]
                        for j in range(4):
                            g[9 + b, h, j // 2, j % 2] = res[j * n : (j + 1) * n]
                    groups[5 + b].start()

    for i in range(7, 10):
        load(i, *loads[i]).wait()

    gain0 = gains[0:1, :].astype(F32)
    rows_total = sm.shape[1]
    sm[0, 0:HEAD_ROWS, :] = small[...]
    sums = rows_total - HEAD_ROWS
    here = 4 * k + z
    lanes = iota((1, width), 1)
    scratch = []

    @pl.loop(0, toks // blk)
    def _(b):
        rows = pl.ds(pl.multiple_of(b * blk, blk), blk)
        raw = mm_nt(dqkv[rows, :], wmv[...])
        v = sv[rows, :]
        cen = v - jnp.mean(v, axis=-1, keepdims=True)
        inv = lax.rsqrt(jnp.mean(cen * cen, axis=-1, keepdims=True) + EPS)
        unit = cen * inv
        gr = raw * gain0
        centred = (
            gr - jnp.mean(gr, axis=-1, keepdims=True)
            - unit * jnp.mean(gr * unit, axis=-1, keepdims=True)
        )
        grad = gm[rows, :] + centred * inv
        igv[rows, :] = grad.astype(BF)
        sm[0, 11:12, :] += jnp.sum(raw * unit, axis=0, keepdims=True)
        sm[0, 12:13, :] += jnp.sum(raw, axis=0, keepdims=True)
        sm[0, 13:14, :] += jnp.sum(grad, axis=0, keepdims=True)

    swap_start(i_at, lambda s: ihome.at[s], isend, irecv)
    square = jnp.sum(small[8:9, :]) * (1.0 / (2 * toks * width))
    sm[0, 8:9, :] = jnp.where(lanes == here, square, 0.0)
    first_chip = z == 0
    for row, source in ((9, ts), (10, buckets)):
        a, b = source[0].astype(F32), source[1].astype(F32)
        line = jnp.where(lanes == 2 * d, a, jnp.where(lanes == 2 * d + 1, b, 0.0))
        sm[0, row : row + 1, :] = jnp.where(first_chip, line, jnp.zeros_like(line))
    sm[0, HEAD_ROWS:, :] = jnp.where(iota((sums, 1), 0) == here, sm[0, 13:14, :], 0.0)
    sm[0, 13:14, :] = jnp.zeros((1, width), F32)

    stages = [(flip(d, bit), z) for bit in bits] + [(d, flip(z, 1)), (d, flip(z, 2))]

    def sum_copy(i):
        return pltpu.make_async_remote_copy(
            sm.at[i], sr.at[i], ssend.at[i], srecv.at[i], device_id=stages[i], device_id_type=MESH
        )

    def sum_step(i):
        sum_copy(i).wait_recv()
        sm[i + 1] = sm[i] + sr[i]
        if i + 1 < len(stages):
            sum_copy(i + 1).start()

    sum_copy(0).start()
    waiting = len(stages)
    done = 0
    while any(one.stage < one.STAGES for one in groups) or done < waiting:
        if done < waiting:
            sum_step(done)
            done += 1
        for one in groups:
            if one.stage < one.STAGES:
                one.take()
                if one.stage == one.STAGES:
                    u = pl.ds(one.first, one.count)
                    pltpu.make_async_copy(f.at[u], f_out.at[u], osem.at[one.index]).start()
    total_out[...] = sm[waiting]

    for one in groups:
        one.close()
        u = pl.ds(one.first, one.count)
        pltpu.make_async_copy(f.at[u], f_out.at[u], osem.at[one.index]).wait()
    for i in range(waiting):
        sum_copy(i).wait_send()

    @pl.loop(0, PAIRS)
    def _(p):
        dkv_copy(p).wait_send()

    for s in range(2):
        swap_wait(lambda s: lhome.at[s], lrecv, s)
        swap_wait(lambda s: ihome.at[s], irecv, s)
    swap_sent(l_at, lambda s: lhome.at[s], lsend, lrecv)
    swap_sent(i_at, lambda s: ihome.at[s], isend, irecv)


def run_backward(kept, ts, buckets, wm, gains, dp):
    toks, width = kept["s"].shape
    part = toks // 2
    shard = width // 8
    bits = axis_bits(dp)
    rows = HEAD_ROWS + 2 * dp
    stages = len(bits) + 2
    vm = lambda shape, dtype: pltpu.VMEM(shape, dtype)
    any_ = pl.BlockSpec(memory_space=pl.ANY)
    vmem = pl.BlockSpec(memory_space=pltpu.VMEM)
    smem = pl.BlockSpec(memory_space=pltpu.SMEM)
    dma = lambda *n: pltpu.SemaphoreType.DMA(n)
    count = len(GROUPS)
    return pl.pallas_call(
        functools.partial(backward_kernel, bits, part),
        out_shape=(
            sds((2, part, width), BF), sds((2, part, width), BF), sds((UNITS, shard, width), BF),
            sds((rows, width), F32),
        ),
        in_specs=[smem] * 2 + [any_] * 11 + [vmem] * 2,
        out_specs=(any_, any_, any_, vmem),
        scratch_shapes=[
            vm((toks, width), F32), vm((toks, width), BF), vm((width, toks), BF), vm((PAIRS, toks, PAIR), BF),
            vm((PAIRS, 2, 2 * toks, PAIR), BF), vm((PAIR, toks), F32), vm((toks, width), BF),
            vm((PAIR, toks), F32), vm((toks, width), F32), vm(wm.shape, BF), vm((PAIRS, 2, toks, PAIR), BF),
            vm((PAIRS, 2, toks, PAIR), BF), vm((toks, PAIR), F32), vm((2, toks, PAIR), F32),
            vm((toks, 3 * width), BF), vm((toks, width), BF),
            vm((UNITS, 2, 2, 2, shard, width), BF), vm((UNITS, 2, 2, shard, width), BF),
            vm((UNITS, 2, shard, width), BF), vm((UNITS, shard, width), BF),
            vm((UNITS, shard // 2, width), BF), vm((UNITS, shard // 2, width // 2), BF),
            vm((UNITS, shard, width), BF), vm((stages + 1, rows, width), F32), vm((stages, rows, width), F32),
            dma(2), dma(2), dma(2), dma(2), dma(PAIRS), dma(PAIRS), dma(count, 7), dma(count, 7),
            dma(stages), dma(stages), dma(10), dma(count),
        ],
        compiler_params=pltpu.CompilerParams(
            collective_id=1, has_side_effects=True, vmem_limit_bytes=60 << 20
        ),
        cost_estimate=pl.CostEstimate(flops=16_000_000_000, bytes_accessed=50_000_000, transcendentals=10_000_000),
        name="backward",
    )(
        ts, buckets, kept["lout"], kept["s"], kept["low1"], kept["q"], kept["kv"], kept["ls"], kept["do"],
        kept["dt"], kept["gm"], kept["g"], wm, kept["small"], gains,
    )


def body(
    inputs, cotangent, time_table, timesteps, buckets, mixer_weight, output_weight, up_weight, down_weight,
    norm_gain, norm_shift, output_bias, up_bias,
):
    seqs, part, width = inputs.shape
    dp = lax.axis_size("dp")
    kept = run_forward(
        timesteps, inputs, cotangent, time_table, mixer_weight, output_weight, up_weight, down_weight,
        norm_gain, norm_shift, output_bias, up_bias,
    )
    lhome, ihome, shares, total = run_backward(kept, timesteps, buckets, mixer_weight, norm_gain, dp)
    shares = shares.astype(F32)
    down = shares[0:4].reshape(width // 2, width)
    rest = shares[4:UNITS]
    inner = dp // 8
    if inner > 1:
        teams = [[h * inner + i for i in range(inner)] for h in range(8)]
        scatter = lambda a, axis: lax.psum_scatter(
            a, "dp", scatter_dimension=axis, axis_index_groups=teams, tiled=True
        )
        down, rest = scatter(down, 0), scatter(rest, 1)
    join = lambda a: jnp.concatenate(list(a), axis=-1)
    count = 2 * dp
    columns = width // dp
    steps, places = total[9, :count], total[10, :count]
    sums = lax.dynamic_slice_in_dim(total[HEAD_ROWS:], lax.axis_index("dp") * columns, columns, 1)
    step_hits = (jnp.arange(STEPS, dtype=F32)[:, None] == steps[None, :]).astype(F32)
    table_grad = lax.dot_general(
        step_hits, sums, (((1,), (0,)), ((), ())), precision=lax.Precision.HIGHEST, preferred_element_type=F32
    )
    hits = (jnp.arange(BUCKETS, dtype=F32)[:, None] == places[None, :]).astype(F32)
    return (
        lhome, ihome.astype(F32), join(rest[5:8]), rest[4], join(rest[0:4]), down,
        jnp.stack([total[11], total[0]]), jnp.stack([total[12], total[1]]), total[2:4],
        total[4:8].reshape(-1), table_grad, jnp.sum(hits * total[8:9, :count], axis=1), jnp.sum(hits, axis=1),
    )


def solution(mesh):
    tokens = P("dp", "seq", None)
    return jax.shard_map(
        body,
        mesh=mesh,
        in_specs=(tokens, tokens, P(), P("dp"), P("dp")) + (P(),) * 8,
        out_specs=(tokens, tokens) + (P("dp", None),) * 4 + (P(),) * 4 + (P(None, "dp"), P(), P()),
        check_vma=False,
    )
```

time: 645 us -> 236 us (0.37); the launches traced: 633 us -> 236 us
  Pallas kernels: 0 us -> 217 us
  blocking collectives: 179 us -> 0 us
  waiting for transfers between devices: 140 us -> 0 us
  matrix products: 121 us -> 1.83 us
  local copies, waits for them, and re-layouts: 107 us -> 10 us
  other arithmetic: 56.5 us -> 6.42 us
  starting transfers between devices: 15.9 us -> 0 us
  between operations: 14.5 us -> 0.68 us
    pallas_call x0 -> x2, Pallas kernels: none -> 217 us  [the longest x1 142 us: run_backward(): pl.pallas_call(functools.partial(backward_kernel, bits, part), out_shape=...]
    dot_general x55 -> x1, matrix products: 121 us -> 1.83 us  [body(): lax.dot_general(step_hits, sums, (((1,), (0,)), ((), ())), precision=lax....]
    all_to_all x3 -> x0, waiting for transfers between devices: 83.8 us -> none  [the longest x1 53.9 us: body(): lax.all_to_all(projected, 'seq', split_axis=2, concat_axis=1, tiled=True)]
    all_gather x1 -> x0, blocking collectives: 77.2 us -> none  [body(): lax.all_gather(seq_sums, ('dp', 'seq'), axis=0, tiled=True)]
    all_to_all x1 -> x0, blocking collectives: 63.4 us -> none  [body(): lax.all_to_all(grad_packed, 'seq', split_axis=1, concat_axis=2, tiled=True)]
    reduce_scatter x4 -> x0, waiting for transfers between devices: 56 us -> none  [the longest x1 56 us: body(): lax.psum_scatter(mixer_grad, 'dp', scatter_dimension=0, tiled=True)]
    psum x1 -> x0, blocking collectives: 38.2 us -> none  [body(): lax.psum((jnp.stack([gain_one, gain_two]), jnp.stack([shift_one, shift_tw...]
    reshape x7 -> x2, local copies, waits for them, and re-layouts: 36.5 us -> 1.91 us  [the longest x1 1.3 us: run_forward(): upb.reshape(1, ff)]
  transfers between devices with their start and end apart: 8 -> 0, of which waited for: 4 -> 0; matrix products, arithmetic and copies ran while one was open for 24% -> 0% of each run, Pallas kernels for 0% -> 0%
where the time goes in v1:
time: 236 us
  Pallas kernels  217 us (92%)
  local copies, waits for them, and re-layouts  10 us (4%)
  other arithmetic  6.42 us (3%)
    pallas_call x1, Pallas kernels, run_backward(): pl.pallas_call(functools.partial(backward_kernel, bits, part), out_shape=...  142 us
    pallas_call x1, Pallas kernels, run_forward(): pl.pallas_call(forward_kernel, out_shape=tuple(outs.values()), in_specs=[...  74.9 us

profile of v1, /device:TPU:0, one launch (start us, length us, event | category | flops | bytes accessed | tf_op | source)
XLA Modules:
  0.0 235.7 jit_solution(11123380872348192036)
XLA Ops:
  0.6 1.3 reshape.35.upb
  1.9 74.9 %forward.1 = (bf16[512,768]{1,0:T(8,128)(2,1)}, f32[512,768]{1,0:T(8,128)}, bf16[512,768]{1,0:T(8,128)(2,1)}, bf16[6,512,128]{2,1,0:T(8,128)(2,1)}, bf16[6,2,102...) custom-call(s32[2]{0:T(128)} %ts.3, ...), custom_call_target="tpu_custom_call" | custom-call | flops 16000000000 | bytes 50000000 | tf_op jit(solution)/shard_map/forward/pallas_call | solution.py:360
  76.9 141.7 %backward.1 = (bf16[2,256,768]{2,1,0:T(8,128)(2,1)}, bf16[2,256,768]{2,1,0:T(8,128)(2,1)}, bf16[12,96,768]{2,1,0:T(8,128)(2,1)}, f32[32,768]{1,0:T(8,128)}) custom-call(s32[2]{0:T(128)} %ts.3, s32[2]{0:T(128)} %buckets.1, bf16[512,768]{1,0:T(8,128)(2,1)} %get-tuple-element.28.lout, f32[512,768]{1,0:T(8,128)} %get-tuple-element.29.s_in, ...), custom_call_target="tpu_custom_call" | custom-call | flops 16000000000 | bytes 50000000 | tf_op jit(solution)/shard_map/backward/pallas_call | solution.py:722
  218.7 0.8 slice_bitcast_fusion.8
  219.4 0.7 convert_reduce_fusion
  220.1 0.8 slice.58
  220.9 1.8 fusion
  222.7 0.8 fusion.4
  223.6 0.6 pad_maximum_fusion.2
  224.2 1.8 convert_element_type.11
  226.0 0.9 slice_bitcast_fusion.3
  226.9 0.0 copy-start.2
  226.9 1.1 pad_maximum_fusion
  228.0 1.0 pad_maximum_fusion.1
  228.9 0.0 copy-start
  229.0 0.0 copy-done.2
  229.0 1.3 convert_element_type.10
  230.2 0.8 copy-done
  231.0 0.0 copy-start.1
  231.0 1.1 slice.62
  232.1 0.7 slice.56
  232.8 0.6 reshape.37
  233.5 1.3 slice.55
  234.8 0.0 copy-done.1
  234.8 0.9 copy.27
Async XLA Ops:
  226.9 2.1 copy-start.2
  228.9 2.0 copy-start
  231.0 3.8 %copy-start.1 = (bf16[2,256,768]{2,1,0:T(8,128)(2,1)S(1)}, bf16[2,256,768]{2,1,0:T(8,128)(2,1)}, u32[]{:S(2)}) copy-start(bf16[2,256,768]{2,1,0:T(8,128)(2,1)} %get-tuple-element.75) | copy-start | bytes 2359300

commit v2 on v0

v2 whole, which is shorter than its diff:
```python
import functools
import math

import jax
import jax.numpy as jnp
from jax import lax
from jax.experimental import pallas as pl
from jax.experimental.pallas import tpu as pltpu
from jax.sharding import PartitionSpec as P

HEADS = 12
HEAD_SIZE = 64
PAIRS = HEADS // 2
PAIR = 2 * HEAD_SIZE
STEPS = 2000
BUCKETS = 8
EPS = 1e-05

BF = jnp.bfloat16
F32 = jnp.float32
MESH = pl.DeviceIdType.MESH


def mm(a, b):
    return lax.dot_general(a, b, (((1,), (0,)), ((), ())), preferred_element_type=F32)


def mm_nt(a, b):
    return lax.dot_general(a, b, (((1,), (1,)), ((), ())), preferred_element_type=F32)


def mm_tn(a, b):
    return lax.dot_general(a, b, (((0,), (0,)), ((), ())), preferred_element_type=F32)


def iota(shape, axis):
    return lax.broadcasted_iota(jnp.int32, shape, axis)


def place():
    d, z = lax.axis_index("dp"), lax.axis_index("seq")
    return d, z, lax.rem(d, 2), lax.div(d, 2)


def column_peers():
    d, z, c, k = place()
    found = []
    for off in range(1, 8):
        m = lax.rem(c * 4 + z + off, 8)
        found.append((2 * k + lax.div(m, 4), lax.rem(m, 4)))
    return found


def greet(ids):
    barrier = pltpu.get_barrier_semaphore()
    for one in ids:
        pl.semaphore_signal(barrier, inc=1, device_id=one, device_id_type=MESH)
    pl.semaphore_wait(barrier, len(ids))


def swap_part(i):
    d, z, c, k = place()
    core, chip = lax.div(z, 2), 2 * c + i
    return core, chip, jnp.logical_and(core == c, chip == z), 2 * k + core


def swap_one(i, source, target, send, recv):
    slot = lax.rem(lax.axis_index("seq"), 2)
    core, chip, own, there = swap_part(i)

    @pl.when(own)
    def _():
        pltpu.make_async_copy(source(i), target(slot), recv.at[slot]).start()

    @pl.when(jnp.logical_not(own))
    def _():
        pltpu.make_async_remote_copy(
            source(i), target(slot), send.at[i], recv.at[slot],
            device_id=(there, chip), device_id_type=MESH,
        ).start()


def swap_start(source, target, send, recv):
    for i in range(2):
        swap_one(i, source, target, send, recv)


def swap_wait(target, recv, s):
    pltpu.make_async_copy(target(s), target(s), recv.at[s]).wait()


def swap_sent(source, target, send, recv):
    for i in range(2):
        core, chip, own, there = swap_part(i)

        @pl.when(jnp.logical_not(own))
        def _():
            pltpu.make_async_remote_copy(
                source(i), target(i), send.at[i], recv.at[i],
                device_id=(there, chip), device_id_type=MESH,
            ).wait_send()


def at(i, n):
    return pl.ds(pl.multiple_of(i * n, n), n)


def flip(index, bit):
    return index + bit - 2 * bit * lax.rem(lax.div(index, bit), 2)


def bit_of(index, bit):
    return lax.rem(lax.div(index, bit), 2)


def axis_bits(size):
    found, bit = [], 1
    while bit < size:
        found.append(bit)
        bit *= 2
    return found


def add_into(dst, *parts):
    total = dst[...].astype(F32)
    for one in parts:
        total = total + one[...].astype(F32)
    dst[...] = total.astype(dst.dtype)


class Reduction:
    def __init__(self, index, kind, g, refs, outer):
        self.index, self.kind, self.g = index, kind, g
        r1, r2, r3, r4, r5, out, self.send, self.recv = refs
        self.out = out.at[index]
        r1, r2, r3, r4, r5 = (r.at[index] for r in (r1, r2, r3, r4, r5))
        d, z, _, _ = place()
        b0, b1, b2 = bit_of(d, outer), bit_of(d, 2 * outer), bit_of(d, 4 * outer)
        near, over_x, over_y = (flip(d, outer), z), (flip(d, 2 * outer), z), (flip(d, 4 * outer), z)
        across = (flip(flip(d, 2 * outer), 4 * outer), z)
        rows, cols = g.shape[-2] // 2, g.shape[-1] // 2
        own = g.at[b2, b1, b0]
        self.used, self.stages = 0, []

        def quarter(ref, q):
            return ref.at[at(lax.rem(q, 2), rows), at(lax.div(q, 2), cols)]

        self.step([(g.at[:, :, 1 - b0], r1, near)], [r1], lambda: self.fold(g, r1, b0))
        if kind[0] == "d":
            moves = [(g.at[b2, 1 - b1, b0], r2.at[0], over_x), (g.at[1 - b2, b1, b0], r2.at[1], over_y),
                     (g.at[1 - b2, 1 - b1, b0], r3, across)]
            self.step(moves, [m[1] for m in moves], lambda: add_into(own, r2.at[0], r2.at[1], r3))
        elif kind[0] == "x":
            self.step([(g.at[:, 1 - b1, b0], r2, over_x)], [r2], lambda: self.fold_x(g, r2, b1, b0))
            self.step([(g.at[1 - b2, b1, b0], r3, over_y)], [r3], lambda: add_into(own, r3))
        else:
            self.step([(g.at[1 - b2, :, b0], r2, over_y)], [r2], lambda: self.fold_y(g, r2, b2, b0))
            self.step([(g.at[b2, 1 - b1, b0], r3, over_x)], [r3], lambda: add_into(own, r3))
        if kind[1] == "s":
            slots = [r4.at[:, pl.ds(0, cols)], r4.at[:, pl.ds(cols, cols)], r5]
            there = [lax.rem(z + o, 4) for o in (1, 2, 3)]
            back = [lax.rem(z + 4 - o, 4) for o in (1, 2, 3)]
            moves = [(quarter(own, there[i]), slots[i], (d, there[i])) for i in range(3)]
            self.step(moves, slots, lambda: self.finish(quarter(own, z), quarter(self.out, z), slots))
            mine = quarter(self.out, z)
            self.step([(mine, mine, (d, one)) for one in there], [quarter(self.out, one) for one in back], None)
        else:
            z0, z1 = lax.rem(z, 2), lax.div(z, 2)
            mine, other = at(z0, rows), at(1 - z0, rows)
            left, right = at(z1, cols), at(1 - z1, cols)
            half = own.at[mine]
            one, two = (d, flip(z, 1)), (d, flip(z, 2))
            self.step([(own.at[other], r4, one)], [r4], lambda: add_into(half, r4))
            self.step(
                [(own.at[mine, right], r5, two)], [r5],
                lambda: self.finish(own.at[mine, left], self.out.at[mine, left], [r5]),
            )
            done = self.out.at[mine, left]
            self.step([(done, done, two)], [self.out.at[mine, right]], None)
            done = self.out.at[mine]
            self.step([(done, done, one)], [self.out.at[other]], None)

    def step(self, moves, landing, combine):
        first = self.used
        self.used += len(moves)
        copies = [
            pltpu.make_async_remote_copy(
                src, dst, self.send.at[self.index, first + i], self.recv.at[self.index, first + i],
                device_id=to, device_id_type=MESH,
            )
            for i, (src, dst, to) in enumerate(moves)
        ]
        waits = [
            pltpu.make_async_copy(here, here, self.recv.at[self.index, first + i])
            for i, here in enumerate(landing)
        ]
        self.stages.append((copies, waits, combine))

    def fold(self, g, r, b0):
        @pl.loop(0, 4)
        def _(i):
            y, x = lax.div(i, 2), lax.rem(i, 2)
            add_into(g.at[y, x, b0], r.at[y, x])

    def fold_x(self, g, r, b1, b0):
        @pl.loop(0, 2)
        def _(i):
            add_into(g.at[i, b1, b0], r.at[i])

    def fold_y(self, g, r, b2, b0):
        @pl.loop(0, 2)
        def _(i):
            add_into(g.at[b2, i, b0], r.at[i])

    def finish(self, own, out, parts):
        total = own[...].astype(F32)
        for one in parts:
            total = total + one[...].astype(F32)
        out[...] = total.astype(out.dtype)

    def start(self):
        for copy in self.stages[0][0]:
            copy.start()

    def take(self, stage):
        _, waits, combine = self.stages[stage]
        for one in waits:
            one.wait()
        if combine is not None:
            combine()
        if stage + 1 < len(self.stages):
            for copy in self.stages[stage + 1][0]:
                copy.start()

    def ends(self, stage):
        return stage + 1 == len(self.stages)

    def close(self):
        for copies, _, _ in self.stages:
            for copy in copies:
                copy.wait_send()


KINDS = ("xs", "ys", "xs", "yh", "xh", "yh", "xh", "yh", "dh", "dh", "dh", "xs")
EARLY = 9
UNITS = 12
VECTORS, LOUT, GRAD = 12, 13, 15
SCHEDULE = (
    ((13, 0), (14, 0), (0, 0)),
    ((1, 0),),
    (),
    (),
    ((2, 0),),
    ((3, 0),),
    (),
    ((1, 1),),
    ((5, 0),),
    ((4, 0),),
    ((2, 1), (1, 2)),
    ((5, 1), (7, 0), (1, 3)),
    ((3, 2), (0, 2)),
    ((2, 3), (3, 3), (7, 1)),
    ((2, 4), (7, 2)),
    (),
    ((3, 1), (0, 1)),
    ((2, 2), (6, 0)),
    ((1, 4), (4, 1), (5, 2)),
    ((5, 3), (6, 1), (4, 2), (0, 3), (8, 0)),
    ((3, 4), (4, 3), (5, 4), (6, 2)),
    ((15, 0), (3, 5), (0, 4), (7, 3), (10, 0)),
)
TAIL = (
    (16, 0), (9, 0), (4, 4), (11, 0), (6, 3), (8, 1), (5, 5), (12, 0), (3, 6), (10, 1),
    (7, 4), (9, 1), (8, 2), (11, 1), (5, 6), (12, 1), (4, 5), (10, 2), (6, 4), (9, 2),
    (7, 5), (11, 2), (8, 3), (4, 6), (12, 2), (10, 3), (6, 5), (7, 6), (9, 3), (11, 3),
    (8, 4), (12, 3), (10, 4), (6, 6), (9, 4), (11, 4), (8, 5), (12, 4), (10, 5), (9, 5),
)
HEAD_ROWS = 16
STEP = 768


def sds(shape, dtype):
    return jax.ShapeDtypeStruct(shape, dtype)


def norm_parts(v):
    cen = v - jnp.mean(v, axis=-1, keepdims=True)
    inv = lax.rsqrt(jnp.mean(cen * cen, axis=-1, keepdims=True) + EPS)
    return cen * inv, inv


def norm_back(raw, unit, inv, gain):
    g = raw * gain
    return inv * (
        g - jnp.mean(g, axis=-1, keepdims=True) - unit * jnp.mean(g * unit, axis=-1, keepdims=True)
    )


class Return:
    def __init__(self, i, *refs):
        self.i, self.refs = i, refs

    def take(self, stage):
        swap_one(self.i, *self.refs)


class VectorSum:
    def __init__(self, sm, sr, send, recv, partners):
        self.sm, self.sr = sm, sr
        self.copies = [
            pltpu.make_async_remote_copy(
                sm.at[i % 2], sr.at[i], send.at[i], recv.at[i], device_id=to, device_id_type=MESH
            )
            for i, to in enumerate(partners)
        ]

    def start(self):
        self.copies[0].start()

    def take(self, i):
        self.copies[i].wait_recv()
        if i:
            self.copies[i - 1].wait_send()
        self.sm[(i + 1) % 2] = self.sm[i % 2] + self.sr[i]
        if i + 1 < len(self.copies):
            self.copies[i + 1].start()

    def close(self):
        self.copies[-1].wait_send()


def layer_kernel(
    bits,
    ts, buckets, x, cot, table, wm, wo, wu, wd, gains, shifts, biases, upb,
    lhome, ihome, f_out, total_out,
    xr, cr, embs, embr, kv, dkvr, r1, r2, r3, r4, r5, f, sm, sr,
    low1, q2, mixed, do, gm, lov, g, ls, lst, dt, upg,
    xsend, xrecv, csend, crecv, esend, erecv, ksend, krecv, lsend, lrecv, isend, irecv,
    dsend, drecv, rsend, rrecv, ssend, srecv, wsem, osem,
):
    d, z, c, k = place()
    toks, width = xr.shape
    part = toks // 2
    ff = wu.shape[1]
    blk = toks // 2
    outer = (1 << len(bits)) // 8
    partner = flip(d, 1)
    row_of = lambda ref, i: ref[i : i + 1, :].astype(F32)
    load = lambda i, src, dst: pltpu.make_async_copy(src, dst, wsem.at[i])
    x_at, c_at = lambda s: xr.at[at(s, part)], lambda s: cr.at[at(s, part)]
    l_at = lambda s: lov.at[at(s, part)]
    low_half = iota((1, PAIR), 1) < HEAD_SIZE
    high_half = jnp.logical_not(low_half)
    lane = iota((1, PAIR), 1)
    mine = at(c, toks)

    across = (flip(flip(d, 2 * outer), 4 * outer), z)
    greet(column_peers() + [(flip(d, bit), z) for bit in bits if bit > 1] + [across])
    swap_start(lambda i: x.at[i], x_at, xsend, xrecv)
    refs = (r1, r2, r3, r4, r5, f, rsend, rrecv)
    units = {i: Reduction(i, KINDS[i], g.at[i], refs, outer) for i in range(EARLY)}
    for i in range(2):
        units[LOUT + i] = Return(i, l_at, lambda s: lhome.at[s], lsend, lrecv)
    plan = iter(SCHEDULE)

    def point():
        for one, stage in next(plan):
            units[one].take(stage)

    def points(count, index):
        for i, row in enumerate([next(plan) for _ in range(count)]):
            if row:

                @pl.when(index == i)
                def _():
                    for one, stage in row:
                        units[one].take(stage)

    def kv_copy(p):
        return pltpu.make_async_remote_copy(
            kv.at[p, :, mine], kv.at[p, :, mine], ksend.at[p], krecv.at[p],
            device_id=(partner, z), device_id_type=MESH,
        )

    def project(wmv, tabv):
        load(1, wm, wmv).start()
        load(0, table, tabv).start()
        load(0, table, tabv).wait()
        row, col = iota((16, tabv.shape[0]), 0), iota((16, tabv.shape[0]), 1)
        wanted = jnp.where(row == 0, ts[0], ts[1])
        hits = jnp.where(jnp.logical_and(col == wanted, row < 2), 1.0, 0.0).astype(BF)
        picked = mm(hits, tabv[...])
        for i in range(2):
            embs[i] = jnp.broadcast_to(picked[i : i + 1], (16, width)).astype(BF)
        swap_start(lambda i: embs.at[i], lambda s: embr.at[s], esend, erecv)
        for s in range(2):
            swap_wait(lambda s: embr.at[s], erecv, s)
        gain, shift = row_of(gains, 0), row_of(shifts, 0)
        for s in range(2):
            swap_wait(x_at, xrecv, s)
            emb = embr[s][0:1, :].astype(F32)

            @pl.loop(0, part // 128)
            def _(b):
                rows = pl.ds(pl.multiple_of(s * part + b * 128, 128), 128)
                unit, _ = norm_parts(xr[rows, :].astype(F32) + emb)
                low1[rows, :] = (unit * gain + shift).astype(BF)

        swap_start(lambda i: cot.at[i], c_at, csend, crecv)
        load(1, wm, wmv).wait()

        @pl.loop(0, PAIRS // 2)
        def _(i):
            res = mm(low1[...], wmv[:, at(i, 6 * PAIR)])
            for j in range(2):
                p = 2 * i + j
                t0, t1, t2 = (res[:, (3 * j + n) * PAIR : (3 * j + n + 1) * PAIR] for n in range(3))
                q2[p] = (jnp.where(low_half, t0, t1).astype(BF) * 0.125).astype(BF)
                kv[p, 0, mine, :] = pltpu.roll(jnp.where(low_half, t2, t0), HEAD_SIZE, 1).astype(BF)
                kv[p, 1, mine, :] = jnp.where(low_half, t1, t2).astype(BF)
                kv_copy(p).start()

    def attend():
        @pl.loop(0, PAIRS)
        def _(p):
            kv_copy(p).wait_recv()
            q, keys, vals = q2[p], kv[p, 0], kv[p, 1]
            scores = [mm_nt(jnp.where(half, q, jnp.zeros_like(q)), keys) for half in (low_half, high_half)]
            tops = [jnp.max(s, axis=-1, keepdims=True) for s in scores]
            powers = [jnp.exp(s - top) for s, top in zip(scores, tops)]
            lows = [e.astype(BF) for e in powers]
            totals = [jnp.sum(e, axis=-1, keepdims=True) for e in powers]
            outs = [mm(e, vals) * (1.0 / total) for e, total in zip(lows, totals)]
            sums = [top + jnp.log(total) for top, total in zip(tops, totals)]
            mixed[:, at(p, PAIR)] = jnp.where(low_half, *outs).astype(BF)
            ls[...] = jnp.where(lane == 2 * p, sums[0], jnp.where(lane == 2 * p + 1, sums[1], ls[...]))

        lst[...] = ls[...].T

    def feed(wov, wuv, wdv, mid, low2, low2t, hid, rl):
        load(2, wo, wov).wait()
        gain, shift, bias = row_of(gains, 1), row_of(shifts, 1), row_of(biases, 0)

        @pl.loop(0, 2)
        def _(b):
            rows = at(b, blk)
            v = xr[rows, :].astype(F32) + embr[b][0:1, :].astype(F32)
            v = v + mm(mixed[rows, :], wov[...]) + bias
            mid[rows, :] = v
            low2[rows, :] = (norm_parts(v)[0] * gain + shift).astype(BF)

        low2t[...] = low2[...].T
        load(3, wu, wuv).wait()
        load(4, wd, wdv).wait()
        for s in range(2):
            swap_wait(c_at, crecv, s)

        @pl.loop(0, ff // STEP)
        def _(j):
            cols = at(j, STEP)
            r = mm(low2[...], wuv[:, cols]) + upb[:, cols].astype(F32)
            back = mm_nt(cr[...], wdv[cols, :])
            half = 0.5 * (1.0 + lax.erf(r * math.sqrt(0.5)))
            bell = jnp.exp(r * r * -0.5) * (1.0 / math.sqrt(2.0 * math.pi))
            hid[:, cols] = (r * half).astype(BF)
            low = (back * (half + r * bell)).astype(BF)
            rl[:, cols] = low
            upg[:, cols] = jnp.sum(low.astype(F32), axis=0, keepdims=True)

        n = g.shape[-2]

        @pl.loop(0, 4)
        def _(j):
            res = mm_tn(hid[:, at(j, width)], cr[...]).astype(BF)
            for s in range(2):
                for i in range(4):
                    first = (4 * s + i) * n
                    g[i, lax.div(j, 2), lax.rem(j, 2), s] = res[first : first + n]

        for i in range(4):
            units[i].start()
        fin = mid[...] + mm(hid[...], wdv[...]) + row_of(biases, 1)
        lov[...] = fin.astype(BF)
        sm[0, 8:9, :] = jnp.sum(fin * fin, axis=0, keepdims=True)
        point()

        @pl.loop(0, 4)
        def _(j):
            res = mm(low2t[...], rl[:, at(j, width)]).astype(BF)
            for i in range(8):
                g[4 + j, i // 4, (i // 2) % 2, i % 2] = res[i * n : (i + 1) * n]
            for i in range(4):

                @pl.when(j == i)
                def _():
                    units[4 + i].start()

            points(4, j)

        gm[...] = mm_nt(rl[...], wuv[...])
        point()

        @pl.loop(0, toks // 128)
        def _(b):
            rows = at(b, 128)
            unit, inv = norm_parts(mid[rows, :])
            raw = gm[rows, :]
            ct = cr[rows, :].astype(F32)
            grad = ct + norm_back(raw, unit, inv, gain)
            gm[rows, :] = grad
            sm[0, 0:1, :] += jnp.sum(raw * unit, axis=0, keepdims=True)
            sm[0, 1:2, :] += jnp.sum(raw, axis=0, keepdims=True)
            sm[0, 2:3, :] += jnp.sum(grad.astype(BF).astype(F32), axis=0, keepdims=True)
            sm[0, 3:4, :] += jnp.sum(ct, axis=0, keepdims=True)

        for i in range(4):
            sm[0, 4 + i : 5 + i, :] = upg[:, i * width : (i + 1) * width]
        point()
        res = mm_tn(mixed[...], gm[...].astype(BF)).astype(BF)
        for i in range(8):
            g[8, i // 4, (i // 2) % 2, i % 2] = res[i * n : (i + 1) * n]
        units[8].start()
        point()
        fold = lax.div(iota((PAIR, width), 1), HEAD_SIZE) == iota((PAIR, width), 0)
        fold = jnp.where(fold, 1.0, 0.0).astype(BF)
        dout = mm_nt(gm[...].astype(BF), wov[...]).astype(BF)
        do[...] = dout
        prod = dout.astype(F32) * mixed[...].astype(F32)
        high = prod.astype(BF)
        rest = (prod - high.astype(F32)).astype(BF)
        dt[...] = mm_nt(fold, high) + mm_nt(fold, rest)
        point()

    def forward(wov, wuv, wdv):
        load(2, wo, wov).start()
        load(3, wu, wuv).start()
        load(4, wd, wdv).start()
        sm[0] = jnp.zeros_like(sm[0])
        pl.run_scoped(project, pltpu.VMEM(wm.shape, BF), pltpu.VMEM(table.shape, BF))
        attend()
        pl.run_scoped(
            functools.partial(feed, wov, wuv, wdv),
            pltpu.VMEM((toks, width), F32), pltpu.VMEM((toks, width), BF), pltpu.VMEM((width, toks), BF),
            pltpu.VMEM((toks, ff), BF), pltpu.VMEM((toks, ff), BF),
        )

    pl.run_scoped(forward, pltpu.VMEM(wo.shape, BF), pltpu.VMEM(wu.shape, BF), pltpu.VMEM(wd.shape, BF))

    def backward(wmv, low1t, late_g, dkvs, dqa, dqkv, igv):
        load(5, wm, wmv).start()
        low1t[...] = low1[...].T
        for i in range(EARLY, UNITS):
            units[i] = Reduction(i, KINDS[i], late_g.at[i - EARLY], refs, outer)
        i_at = lambda s: igv.at[at(s, part)]

        def dkv_copy(p):
            return pltpu.make_async_remote_copy(
                dkvs.at[p], dkvr.at[p], dsend.at[p], drecv.at[p],
                device_id=(partner, z), device_id_type=MESH,
            )

        halves = (low_half, high_half)

        def attend_back(p, base):
            rows = pl.ds(pl.multiple_of(base, toks), toks)
            keys, vals = kv[p, 0, rows, :], kv[p, 1, rows, :]
            q, dout = q2[p], do[:, at(p, PAIR)]
            dks, dvs, dqs = [], [], []
            for h, half in enumerate(halves):
                kh = jnp.where(half, keys, jnp.zeros_like(keys))
                vh = jnp.where(half, vals, jnp.zeros_like(vals))
                probs = jnp.exp(mm_nt(kh, q) - lst[pl.ds(2 * p + h, 1), :])
                ds = (probs * (mm_nt(vh, dout) - dt[pl.ds(2 * p + h, 1), :])).astype(BF)
                dvs.append(mm(probs.astype(BF), dout))
                dks.append(mm(ds, q))
                dqs.append(mm_tn(ds, kh))
            return jnp.where(low_half, *dks), jnp.where(low_half, *dvs), dqs[0] + dqs[1]

        @pl.loop(0, PAIRS)
        def _(p):
            dk, dv, dq = attend_back(p, (1 - c) * toks)
            dkvs[p, 0] = dk.astype(BF)
            dkvs[p, 1] = dv.astype(BF)
            dqa[...] = dq
            dkv_copy(p).start()
            points(PAIRS, p)
            dk, dv, dq = attend_back(p, c * toks)
            dkv_copy(p).wait_recv()
            dq = (dq + dqa[...]) * 0.125
            dk = pltpu.roll(dk + dkvr[p, 0].astype(F32), HEAD_SIZE, 1)
            dv = dv + dkvr[p, 1].astype(F32)
            dqkv[:, at(3 * p, PAIR)] = jnp.where(low_half, dq, dk).astype(BF)
            dqkv[:, at(3 * p + 1, PAIR)] = jnp.where(low_half, dv, dq).astype(BF)
            dqkv[:, at(3 * p + 2, PAIR)] = jnp.where(low_half, dk, dv).astype(BF)

            @pl.when(lax.rem(p, 2) == 1)
            def _():
                b = lax.div(p, 2)
                n = g.shape[-2]
                res = mm(low1t[...], dqkv[:, at(b, width)]).astype(BF)
                for j in range(8):
                    late_g[b, j // 4, (j // 2) % 2, j % 2] = res[j * n : (j + 1) * n]
                for i in range(3):

                    @pl.when(b == i)
                    def _():
                        units[EARLY + i].start()

            points(PAIRS, p)

        load(5, wm, wmv).wait()
        gain0 = row_of(gains, 0)
        here = 4 * k + z
        lanes = iota((1, width), 1)

        @pl.loop(0, 2)
        def _(b):
            rows = at(b, blk)
            raw = mm_nt(dqkv[rows, :], wmv[...])
            unit, inv = norm_parts(xr[rows, :].astype(F32) + embr[b][0:1, :].astype(F32))
            grad = gm[rows, :] + norm_back(raw, unit, inv, gain0)
            igv[rows, :] = grad.astype(BF)
            sm[0, 11:12, :] += jnp.sum(raw * unit, axis=0, keepdims=True)
            sm[0, 12:13, :] += jnp.sum(raw, axis=0, keepdims=True)
            sm[0, 13:14, :] += jnp.sum(grad, axis=0, keepdims=True)

        square = jnp.sum(sm[0, 8:9, :]) * (1.0 / (2 * toks * width))
        sm[0, 8:9, :] = jnp.where(lanes == here, square, 0.0)
        for row, source in ((9, ts), (10, buckets)):
            first, second = source[0].astype(F32), source[1].astype(F32)
            line = jnp.where(lanes == 2 * d, first, jnp.where(lanes == 2 * d + 1, second, 0.0))
            sm[0, row : row + 1, :] = jnp.where(z == 0, line, jnp.zeros_like(line))
        sums = sm.shape[1] - HEAD_ROWS
        sm[0, HEAD_ROWS:, :] = jnp.where(iota((sums, 1), 0) == here, sm[0, 13:14, :], 0.0)
        stages = [(flip(d, bit), z) for bit in bits] + [(d, flip(z, 1)), (d, flip(z, 2))]

        vectors = VectorSum(sm, sr, ssend, srecv, stages)
        units[VECTORS] = vectors
        for i in range(2):
            units[GRAD + i] = Return(i, i_at, lambda s: ihome.at[s], isend, irecv)
        vectors.start()

        def put(i):
            return pltpu.make_async_copy(f.at[i], f_out.at[i], osem.at[i])

        point()
        for one, stage in TAIL:
            units[one].take(stage)
            if one < UNITS and units[one].ends(stage):
                put(one).start()
        for one in range(UNITS):
            if not any(i == one and units[one].ends(stage) for i, stage in TAIL):
                put(one).start()
        extra = len(stages) - 5
        for i in range(extra):
            vectors.take(5 + i)
        result = pltpu.make_async_copy(sm.at[len(stages) % 2], total_out, wsem.at[0])
        result.start()
        for i in range(UNITS + 1):
            units[i].close()
        for i in range(UNITS):
            put(i).wait()
        result.wait()

        @pl.loop(0, PAIRS)
        def _(p):
            kv_copy(p).wait_send()
            dkv_copy(p).wait_send()

        for s in range(2):
            swap_wait(lambda s: lhome.at[s], lrecv, s)
            swap_wait(lambda s: ihome.at[s], irecv, s)
        swap_sent(lambda i: x.at[i], x_at, xsend, xrecv)
        swap_sent(lambda i: cot.at[i], c_at, csend, crecv)
        swap_sent(lambda i: embs.at[i], lambda s: embr.at[s], esend, erecv)
        swap_sent(l_at, lambda s: lhome.at[s], lsend, lrecv)
        swap_sent(i_at, lambda s: ihome.at[s], isend, irecv)

    shard = g.shape[-2]
    pl.run_scoped(
        backward,
        pltpu.VMEM(wm.shape, BF), pltpu.VMEM((width, toks), BF),
        pltpu.VMEM((UNITS - EARLY, 2, 2, 2, shard, width), BF), pltpu.VMEM((PAIRS, 2, toks, PAIR), BF),
        pltpu.VMEM((toks, PAIR), F32), pltpu.VMEM((toks, 3 * width), BF),
        pltpu.VMEM((toks, width), BF),
    )


def run_layer(ts, buckets, x, cot, table, wm, wo, wu, wd, gains, shifts, biases, upb, dp):
    _, part, width = x.shape
    toks = 2 * part
    ff = wu.shape[1]
    shard = width // 8
    bits = axis_bits(dp)
    rows = HEAD_ROWS + 2 * dp
    stages = len(bits) + 2
    vm = lambda shape, dtype: pltpu.VMEM(shape, dtype)
    any_ = pl.BlockSpec(memory_space=pl.ANY)
    vmem = pl.BlockSpec(memory_space=pltpu.VMEM)
    smem = pl.BlockSpec(memory_space=pltpu.SMEM)
    dma = lambda *n: pltpu.SemaphoreType.DMA(n)
    return pl.pallas_call(
        functools.partial(layer_kernel, bits),
        out_shape=(
            sds((2, part, width), BF), sds((2, part, width), BF), sds((UNITS, shard, width), BF),
            sds((rows, width), F32),
        ),
        in_specs=[smem] * 2 + [any_] * 7 + [vmem] * 4,
        out_specs=(any_,) * 4,
        scratch_shapes=[
            vm((toks, width), BF), vm((toks, width), BF), vm((2, 16, width), BF), vm((2, 16, width), BF),
            vm((PAIRS, 2, 2 * toks, PAIR), BF), vm((PAIRS, 2, toks, PAIR), BF),
            vm((UNITS, 2, 2, shard, width), BF), vm((UNITS, 2, shard, width), BF), vm((UNITS, shard, width), BF),
            vm((UNITS, shard // 2, width), BF), vm((UNITS, shard // 2, width // 2), BF),
            vm((UNITS, shard, width), BF), vm((2, rows, width), F32), vm((stages, rows, width), F32),
            vm((toks, width), BF), vm((PAIRS, toks, PAIR), BF), vm((toks, width), BF), vm((toks, width), BF),
            vm((toks, width), F32), vm((toks, width), BF), vm((EARLY, 2, 2, 2, shard, width), BF),
            vm((toks, PAIR), F32), vm((PAIR, toks), F32), vm((PAIR, toks), F32), vm((1, ff), F32),
            dma(2), dma(2), dma(2), dma(2), dma(2), dma(2), dma(PAIRS), dma(PAIRS),
            dma(2), dma(2), dma(2), dma(2), dma(PAIRS), dma(PAIRS), dma(UNITS, 10), dma(UNITS, 10),
            dma(stages), dma(stages), dma(6), dma(UNITS),
        ],
        compiler_params=pltpu.CompilerParams(
            collective_id=0, has_side_effects=True, vmem_limit_bytes=127 << 19
        ),
        cost_estimate=pl.CostEstimate(
            flops=32_000_000_000, bytes_accessed=60_000_000, transcendentals=20_000_000
        ),
        name="layer",
    )(ts, buckets, x, cot, table, wm, wo, wu, wd, gains, shifts, biases, upb.reshape(1, ff))


def finish_kernel(
    lhome, ihome_in, f_in, total_in, layer_out, input_grad, mixer, output, up, down, gains, shifts, biases, upb,
    table, norms, counts, ihome, f, total, sem,
):
    n, width = f.shape[1:]
    columns, step_count = table.shape
    copies = [
        pltpu.make_async_copy(src, dst, sem.at[i])
        for i, (src, dst) in enumerate(((total_in, total), (f_in, f), (ihome_in, ihome), (lhome, layer_out)))
    ]
    for one in copies:
        one.start()
    copies[0].wait()
    for i in range(4):
        upb[pl.ds(i * width, width)] = total[4 + i, :]
    for i, row in enumerate((11, 0)):
        gains[i : i + 1, :] = total[row : row + 1, :]
        shifts[i : i + 1, :] = total[row + 1 : row + 2, :]
    biases[...] = total[2:4, :]
    count = total.shape[0] - HEAD_ROWS
    first = lax.axis_index("dp") * columns
    chosen = iota((width, columns), 0) == iota((width, columns), 1) + first
    chosen = jnp.where(chosen, 1.0, 0.0).astype(BF)
    steps = total[9:10, :count]
    hits = jnp.where(iota((step_count, count), 0).astype(F32) == steps, 1.0, 0.0).astype(BF)
    here = iota((BUCKETS, count), 0).astype(F32) == total[10:11, :count]
    here = jnp.where(here, 1.0, 0.0).astype(BF)
    rest, grad = total[HEAD_ROWS:, :], 0.0
    means = jnp.where(iota((8, count), 0) == 0, total[8:9, :count], 1.0)
    norm = 0.0
    for _ in range(3):
        piece = rest.astype(BF)
        rest = rest - piece.astype(F32)
        part = mm(piece, chosen).astype(BF)
        grad = grad + lax.dot_general(part, hits, (((0,), (1,)), ((), ())), preferred_element_type=F32)
        piece = means.astype(BF)
        means = means - piece.astype(F32)
        norm = norm + mm_nt(piece, here)
    table[...] = grad
    norms[...] = norm[0, :]
    counts[...] = norm[1, :]
    copies[1].wait()
    for i in range(4):
        down[i * n : (i + 1) * n, :] = f[i].astype(F32)
        up[:, i * width : (i + 1) * width] = f[4 + i].astype(F32)
    output[...] = f[8].astype(F32)
    for i in range(3):
        mixer[:, i * width : (i + 1) * width] = f[9 + i].astype(F32)
    copies[2].wait()
    input_grad[...] = ihome[...].astype(F32)
    copies[3].wait()


def run_finish(lhome, ihome, f, total, dp, steps):
    n, width = f.shape[1:]
    outs = [
        sds(lhome.shape, BF), sds(ihome.shape, F32), sds((n, 3 * width), F32), sds((n, width), F32),
        sds((n, 4 * width), F32), sds((4 * n, width), F32), sds((2, width), F32), sds((2, width), F32),
        sds((2, width), F32), sds((4 * width,), F32), sds((width // dp, steps), F32), sds((BUCKETS,), F32),
        sds((BUCKETS,), F32),
    ]
    vmem, any_ = pl.BlockSpec(memory_space=pltpu.VMEM), pl.BlockSpec(memory_space=pl.ANY)
    res = pl.pallas_call(
        finish_kernel,
        out_shape=outs,
        in_specs=[any_] * 4,
        out_specs=[vmem] * len(outs),
        scratch_shapes=[
            pltpu.VMEM(ihome.shape, BF), pltpu.VMEM(f.shape, f.dtype), pltpu.VMEM(total.shape, F32),
            pltpu.SemaphoreType.DMA((4,)),
        ],
        compiler_params=pltpu.CompilerParams(vmem_limit_bytes=60 << 20),
        name="finish",
    )(lhome, ihome, f, total)
    return (*res[:10], res[10].T, *res[11:])


def body(
    inputs, cotangent, time_table, timesteps, buckets, mixer_weight, output_weight, up_weight, down_weight,
    norm_gain, norm_shift, output_bias, up_bias,
):
    width = inputs.shape[-1]
    dp = lax.axis_size("dp")
    lhome, ihome, shares, total = run_layer(
        timesteps, buckets, inputs, cotangent, time_table, mixer_weight, output_weight, up_weight,
        down_weight, norm_gain, norm_shift, output_bias, up_bias, dp,
    )
    inner = dp // 8
    if inner > 1:
        teams = [[h * inner + i for i in range(inner)] for h in range(8)]
        scatter = lambda a, axis: lax.psum_scatter(
            a, "dp", scatter_dimension=axis, axis_index_groups=teams, tiled=True
        )
        shares = shares.astype(F32)
        down, rest = scatter(shares[0:4].reshape(width // 2, width), 0), scatter(shares[4:UNITS], 1)
        shares = jnp.concatenate([down.reshape((4,) + rest.shape[1:]), rest])
    return run_finish(lhome, ihome, shares, total, dp, time_table.shape[0])


def solution(mesh):
    tokens = P("dp", "seq", None)
    return jax.shard_map(
        body,
        mesh=mesh,
        in_specs=(tokens, tokens, P(), P("dp"), P("dp")) + (P(),) * 8,
        out_specs=(tokens, tokens) + (P("dp", None),) * 4 + (P(),) * 4 + (P(None, "dp"), P(), P()),
        check_vma=False,
    )
```

time: 645 us -> 166 us (0.26); the launches traced: 633 us -> 166 us
  blocking collectives: 179 us -> 0 us
  Pallas kernels: 0 us -> 164 us
  waiting for transfers between devices: 140 us -> 0 us
  matrix products: 121 us -> 0 us
  local copies, waits for them, and re-layouts: 107 us -> 1.3 us
  other arithmetic: 56.5 us -> 0 us
  starting transfers between devices: 15.9 us -> 0 us
  between operations: 14.5 us -> 0.81 us
    pallas_call x0 -> x2, Pallas kernels: none -> 164 us  [the longest x1 159 us: run_layer(): pl.pallas_call(functools.partial(layer_kernel, bits), out_shape=(sds((2,...]
    dot_general x55 -> x0, matrix products: 121 us -> none  [the longest x22 51.7 us: contract_cols(): lax.dot_general(left_side, right_side, (((1,), (1,)), ((), ())), preferre...]
    all_to_all x3 -> x0, waiting for transfers between devices: 83.8 us -> none  [the longest x1 53.9 us: body(): lax.all_to_all(projected, 'seq', split_axis=2, concat_axis=1, tiled=True)]
    all_gather x1 -> x0, blocking collectives: 77.2 us -> none  [body(): lax.all_gather(seq_sums, ('dp', 'seq'), axis=0, tiled=True)]
    all_to_all x1 -> x0, blocking collectives: 63.4 us -> none  [body(): lax.all_to_all(grad_packed, 'seq', split_axis=1, concat_axis=2, tiled=True)]
    reduce_scatter x4 -> x0, waiting for transfers between devices: 56 us -> none  [the longest x1 56 us: body(): lax.psum_scatter(mixer_grad, 'dp', scatter_dimension=0, tiled=True)]
    psum x1 -> x0, blocking collectives: 38.2 us -> none  [body(): lax.psum((jnp.stack([gain_one, gain_two]), jnp.stack([shift_one, shift_tw...]
    reshape x7 -> x1, local copies, waits for them, and re-layouts: 36.5 us -> 1.3 us  [run_layer(): upb.reshape(1, ff)]
  transfers between devices with their start and end apart: 8 -> 0, of which waited for: 4 -> 0; matrix products, arithmetic and copies ran while one was open for 24% -> 0% of each run, Pallas kernels for 0% -> 0%
where the time goes in v2:
time: 166 us
  Pallas kernels  164 us (99%)
    pallas_call x1, Pallas kernels, run_layer(): pl.pallas_call(functools.partial(layer_kernel, bits), out_shape=(sds((2,...  159 us
    pallas_call x1, Pallas kernels, run_finish(): pl.pallas_call(finish_kernel, out_shape=outs, in_specs=[any_] * 4, out_sp...  5.14 us

profile of v2, /device:TPU:0, one launch (start us, length us, event | category | flops | bytes accessed | tf_op | source)
XLA Modules:
  0.0 166.1 jit_solution(1857664047774063421)
XLA Ops:
  0.6 1.3 reshape.29.upb
  1.9 158.8 %layer.1 = (bf16[2,256,768]{2,1,0:T(8,128)(2,1)}, bf16[2,256,768]{2,1,0:T(8,128)(2,1)}, bf16[12,96,768]{2,1,0:T(8,128)(2,1)}, f32[32,768]{1,0:T(8,128)}) custom-call(s32[2]{0:T(128)} %ts.1, s32[2]{0:T(128)} %buckets.1, bf16[2,256,768]{2,1,0:T(8,128)(2,1)} %x.1, bf16[2,256,768]{2,1,0:T(8,128)(2,1)} %cot.1, bf16[2000,768]{1,0:T(8,128)(2,1)} %table.1, ...), custom_call_target="tpu_custom_call" | custom-call | flops 32000000000 | bytes 60000000 | tf_op jit(solution)/shard_map/layer/pallas_call | solution.py:702
  160.8 5.1 %finish.1 = (bf16[2,256,768]{2,1,0:T(8,128)(2,1)}, f32[2,256,768]{2,1,0:T(8,128)}, f32[96,2304]{1,0:T(8,128)}, f32[96,768]{1,0:T(8,128)}, f32[96,3072]{1,0:T(8,1...) custom-call(bf16[2,256,768]{2,1,0:T(8,128)(2,1)} %get-tuple-element., ...), custom_call_target="tpu_custom_call" | custom-call | tf_op jit(solution)/shard_map/finish/pallas_call | solution.py:795

commit v3 on v2

--- a/solution.py
+++ b/solution.py
@@ -241,39 +241,43 @@
                 copy.wait_send()
 
 
-KINDS = ("xs", "ys", "xs", "yh", "xh", "yh", "xh", "yh", "dh", "dh", "dh", "xs")
+KINDS = ("xs", "yh", "xh", "yh", "xh", "xs", "xh", "ys", "dh", "dh", "dh", "ds")
 EARLY = 9
 UNITS = 12
 VECTORS, LOUT, GRAD = 12, 13, 15
 SCHEDULE = (
-    ((13, 0), (14, 0), (0, 0)),
+    ((13, 0),),
+    ((0, 0), (14, 0)),
     ((1, 0),),
     (),
     (),
     ((2, 0),),
     ((3, 0),),
     (),
+    (),
     ((1, 1),),
+    ((0, 1),),
     ((5, 0),),
-    ((4, 0),),
-    ((2, 1), (1, 2)),
-    ((5, 1), (7, 0), (1, 3)),
-    ((3, 2), (0, 2)),
-    ((2, 3), (3, 3), (7, 1)),
-    ((2, 4), (7, 2)),
+    ((2, 1),),
+    ((7, 0),),
     (),
-    ((3, 1), (0, 1)),
-    ((2, 2), (6, 0)),
-    ((1, 4), (4, 1), (5, 2)),
-    ((5, 3), (6, 1), (4, 2), (0, 3), (8, 0)),
-    ((3, 4), (4, 3), (5, 4), (6, 2)),
-    ((15, 0), (3, 5), (0, 4), (7, 3), (10, 0)),
+    ((0, 3), (3, 2)),
+    ((5, 2), (6, 0)),
+    ((7, 2), (10, 0)),
+    ((3, 4), (4, 2)),
+    ((1, 2), (0, 2), (3, 1)),
+    ((2, 2), (1, 3), (5, 1), (4, 0)),
+    ((2, 3), (1, 4), (7, 1)),
+    ((2, 4), (0, 4), (3, 3), (1, 5), (4, 1)),
+    ((5, 3), (2, 5), (1, 6)),
+    ((7, 3),),
+    ((15, 0), (2, 6), (5, 4), (3, 5), (4, 3), (6, 1)),
 )
 TAIL = (
-    (16, 0), (9, 0), (4, 4), (11, 0), (6, 3), (8, 1), (5, 5), (12, 0), (3, 6), (10, 1),
-    (7, 4), (9, 1), (8, 2), (11, 1), (5, 6), (12, 1), (4, 5), (10, 2), (6, 4), (9, 2),
-    (7, 5), (11, 2), (8, 3), (4, 6), (12, 2), (10, 3), (6, 5), (7, 6), (9, 3), (11, 3),
-    (8, 4), (12, 3), (10, 4), (6, 6), (9, 4), (11, 4), (8, 5), (12, 4), (10, 5), (9, 5),
+    (16, 0), (9, 0), (8, 0), (11, 0), (12, 0), (10, 1), (7, 4), (6, 2), (3, 6), (9, 1),
+    (4, 4), (8, 1), (10, 2), (6, 3), (9, 2), (4, 5), (12, 1), (8, 2), (11, 1), (10, 3),
+    (6, 4), (9, 3), (12, 2), (4, 6), (8, 3), (11, 2), (10, 4), (6, 5), (12, 3), (9, 4),
+    (8, 4), (10, 5), (11, 3), (6, 6), (9, 5), (12, 4), (8, 5),
 )
 HEAD_ROWS = 16
 STEP = 768
@@ -334,7 +338,7 @@
     ts, buckets, x, cot, table, wm, wo, wu, wd, gains, shifts, biases, upb,
     lhome, ihome, f_out, total_out,
     xr, cr, embs, embr, kv, dkvr, r1, r2, r3, r4, r5, f, sm, sr,
-    low1, q2, mixed, do, gm, lov, g, ls, lst, dt, upg,
+    low1, q2, mixed, do, gm, lov, g, ls, lst, dt, upg, upv,
     xsend, xrecv, csend, crecv, esend, erecv, ksend, krecv, lsend, lrecv, isend, irecv,
     dsend, drecv, rsend, rrecv, ssend, srecv, wsem, osem,
 ):
@@ -355,6 +359,7 @@
     mine = at(c, toks)
 
     across = (flip(flip(d, 2 * outer), 4 * outer), z)
+    upv[0, :] = upb[...].astype(F32)
     greet(column_peers() + [(flip(d, bit), z) for bit in bits if bit > 1] + [across])
     swap_start(lambda i: x.at[i], x_at, xsend, xrecv)
     refs = (r1, r2, r3, r4, r5, f, rsend, rrecv)
@@ -451,22 +456,19 @@
 
         low2t[...] = low2[...].T
         load(3, wu, wuv).wait()
+
+        @pl.loop(0, ff // STEP)
+        def _(j):
+            cols = at(j, STEP)
+            r = mm(low2[...], wuv[:, cols]) + upv[:, cols]
+            half = 0.5 * (1.0 + lax.erf(r * math.sqrt(0.5)))
+            bell = jnp.exp(r * r * -0.5) * (1.0 / math.sqrt(2.0 * math.pi))
+            hid[:, cols] = (r * half).astype(BF)
+            rl[:, cols] = (half + r * bell).astype(BF)
+
         load(4, wd, wdv).wait()
         for s in range(2):
             swap_wait(c_at, crecv, s)
-
-        @pl.loop(0, ff // STEP)
-        def _(j):
-            cols = at(j, STEP)
-            r = mm(low2[...], wuv[:, cols]) + upb[:, cols].astype(F32)
-            back = mm_nt(cr[...], wdv[cols, :])
-            half = 0.5 * (1.0 + lax.erf(r * math.sqrt(0.5)))
-            bell = jnp.exp(r * r * -0.5) * (1.0 / math.sqrt(2.0 * math.pi))
-            hid[:, cols] = (r * half).astype(BF)
-            low = (back * (half + r * bell)).astype(BF)
-            rl[:, cols] = low
-            upg[:, cols] = jnp.sum(low.astype(F32), axis=0, keepdims=True)
-
         n = g.shape[-2]
 
         @pl.loop(0, 4)
@@ -483,6 +485,15 @@
         lov[...] = fin.astype(BF)
         sm[0, 8:9, :] = jnp.sum(fin * fin, axis=0, keepdims=True)
         point()
+
+        @pl.loop(0, ff // STEP)
+        def _(j):
+            cols = at(j, STEP)
+            low = (mm_nt(cr[...], wdv[cols, :]) * rl[:, cols].astype(F32)).astype(BF)
+            rl[:, cols] = low
+            upg[:, cols] = jnp.sum(low.astype(F32), axis=0, keepdims=True)
+            points(4, j)
+
 
         @pl.loop(0, 4)
         def _(j):
@@ -715,7 +726,7 @@
             vm((UNITS, shard, width), BF), vm((2, rows, width), F32), vm((stages, rows, width), F32),
             vm((toks, width), BF), vm((PAIRS, toks, PAIR), BF), vm((toks, width), BF), vm((toks, width), BF),
             vm((toks, width), F32), vm((toks, width), BF), vm((EARLY, 2, 2, 2, shard, width), BF),
-            vm((toks, PAIR), F32), vm((PAIR, toks), F32), vm((PAIR, toks), F32), vm((1, ff), F32),
+            vm((toks, PAIR), F32), vm((PAIR, toks), F32), vm((PAIR, toks), F32), vm((1, ff), F32), vm((1, ff), F32),
             dma(2), dma(2), dma(2), dma(2), dma(2), dma(2), dma(PAIRS), dma(PAIRS),
             dma(2), dma(2), dma(2), dma(2), dma(PAIRS), dma(PAIRS), dma(UNITS, 10), dma(UNITS, 10),
             dma(stages), dma(stages), dma(6), dma(UNITS),
@@ -727,21 +738,45 @@
             flops=32_000_000_000, bytes_accessed=60_000_000, transcendentals=20_000_000
         ),
         name="layer",
-    )(ts, buckets, x, cot, table, wm, wo, wu, wd, gains, shifts, biases, upb.reshape(1, ff))
+    )(ts, buckets, x, cot, table, wm, wo, wu, wd, gains, shifts, biases, upb)
 
 
 def finish_kernel(
-    lhome, ihome_in, f_in, total_in, layer_out, input_grad, mixer, output, up, down, gains, shifts, biases, upb,
-    table, norms, counts, ihome, f, total, sem,
+    lhome, ihome_in, f_in, total_in, *refs,
 ):
+    big, small, held = refs[:7], refs[7:13], refs[13:20]
+    layer_out, input_grad, mixer, output, up, down, table = held
+    gains, shifts, biases, upb, norms, counts = small
+    ihome, f, total, sem, done = refs[20:]
     n, width = f.shape[1:]
     columns, step_count = table.shape
-    copies = [
-        pltpu.make_async_copy(src, dst, sem.at[i])
-        for i, (src, dst) in enumerate(((total_in, total), (f_in, f), (ihome_in, ihome), (lhome, layer_out)))
+    copies = [pltpu.make_async_copy(total_in, total, sem.at[0])]
+    copies += [
+        pltpu.make_async_copy(f_in.at[pl.ds(4 * i, 4)], f.at[pl.ds(4 * i, 4)], sem.at[1 + i]) for i in range(3)
     ]
+    copies += [pltpu.make_async_copy(ihome_in, ihome, sem.at[4]), pltpu.make_async_copy(lhome, layer_out, sem.at[5])]
     for one in copies:
         one.start()
+    leave = [pltpu.make_async_copy(src, dst, done.at[i]) for i, (src, dst) in enumerate(zip(held, big))]
+    copies[1].wait()
+    for i in range(4):
+        down[i * n : (i + 1) * n, :] = f[i].astype(F32)
+    leave[5].start()
+    copies[2].wait()
+    for i in range(4):
+        up[:, i * width : (i + 1) * width] = f[4 + i].astype(F32)
+    leave[4].start()
+    copies[4].wait()
+    input_grad[...] = ihome[...].astype(F32)
+    leave[1].start()
+    copies[3].wait()
+    output[...] = f[8].astype(F32)
+    for i in range(3):
+        mixer[:, i * width : (i + 1) * width] = f[9 + i].astype(F32)
+    leave[3].start()
+    leave[2].start()
+    copies[5].wait()
+    leave[0].start()
     copies[0].wait()
     for i in range(4):
         upb[pl.ds(i * width, width)] = total[4 + i, :]
@@ -769,42 +804,34 @@
         means = means - piece.astype(F32)
         norm = norm + mm_nt(piece, here)
     table[...] = grad
+    leave[6].start()
     norms[...] = norm[0, :]
     counts[...] = norm[1, :]
-    copies[1].wait()
-    for i in range(4):
-        down[i * n : (i + 1) * n, :] = f[i].astype(F32)
-        up[:, i * width : (i + 1) * width] = f[4 + i].astype(F32)
-    output[...] = f[8].astype(F32)
-    for i in range(3):
-        mixer[:, i * width : (i + 1) * width] = f[9 + i].astype(F32)
-    copies[2].wait()
-    input_grad[...] = ihome[...].astype(F32)
-    copies[3].wait()
+    for one in leave:
+        one.wait()
 
 
 def run_finish(lhome, ihome, f, total, dp, steps):
     n, width = f.shape[1:]
-    outs = [
+    big = [
         sds(lhome.shape, BF), sds(ihome.shape, F32), sds((n, 3 * width), F32), sds((n, width), F32),
-        sds((n, 4 * width), F32), sds((4 * n, width), F32), sds((2, width), F32), sds((2, width), F32),
-        sds((2, width), F32), sds((4 * width,), F32), sds((width // dp, steps), F32), sds((BUCKETS,), F32),
-        sds((BUCKETS,), F32),
+        sds((n, 4 * width), F32), sds((4 * n, width), F32), sds((width // dp, steps), F32),
     ]
+    small = [sds((2, width), F32)] * 3 + [sds((4 * width,), F32), sds((BUCKETS,), F32), sds((BUCKETS,), F32)]
     vmem, any_ = pl.BlockSpec(memory_space=pltpu.VMEM), pl.BlockSpec(memory_space=pl.ANY)
     res = pl.pallas_call(
         finish_kernel,
-        out_shape=outs,
+        out_shape=big + small,
         in_specs=[any_] * 4,
-        out_specs=[vmem] * len(outs),
-        scratch_shapes=[
+        out_specs=[any_] * len(big) + [vmem] * len(small),
+        scratch_shapes=[pltpu.VMEM(one.shape, one.dtype) for one in big] + [
             pltpu.VMEM(ihome.shape, BF), pltpu.VMEM(f.shape, f.dtype), pltpu.VMEM(total.shape, F32),
-            pltpu.SemaphoreType.DMA((4,)),
+            pltpu.SemaphoreType.DMA((6,)), pltpu.SemaphoreType.DMA((len(big),)),
         ],
         compiler_params=pltpu.CompilerParams(vmem_limit_bytes=60 << 20),
         name="finish",
     )(lhome, ihome, f, total)
-    return (*res[:10], res[10].T, *res[11:])
+    return (*res[:6], *res[7:11], res[6].T, *res[11:])
 
 
 def body(

time: 166 us -> 160 us (0.964)
  Pallas kernels: 164 us -> 159 us
    pallas_call x1, Pallas kernels: 159 us -> 154 us  [run_layer(): pl.pallas_call(functools.partial(layer_kernel, bits), out_shape=(sds((2,...]
where the time goes in v3:
time: 160 us
  Pallas kernels  159 us (99%)
    pallas_call x1, Pallas kernels, run_layer(): pl.pallas_call(functools.partial(layer_kernel, bits), out_shape=(sds((2,...  154 us
    pallas_call x1, Pallas kernels, run_finish(): pl.pallas_call(finish_kernel, out_shape=big + small, in_specs=[any_] * 4,...  4.7 us

profile of v3, /device:TPU:0, one launch (start us, length us, event | category | flops | bytes accessed | tf_op | source)
XLA Modules:
  0.0 159.9 jit_solution(8812032552642465919)
XLA Ops:
  0.6 154.4 %layer.1 = (bf16[2,256,768]{2,1,0:T(8,128)(2,1)}, bf16[2,256,768]{2,1,0:T(8,128)(2,1)}, bf16[12,96,768]{2,1,0:T(8,128)(2,1)}, f32[32,768]{1,0:T(8,128)}) custom-call(s32[2]{0:T(128)} %ts.1, s32[2]{0:T(128)} %buckets.1, bf16[2,256,768]{2,1,0:T(8,128)(2,1)} %x.1, bf16[2,256,768]{2,1,0:T(8,128)(2,1)} %cot.1, bf16[2000,768]{1,0:T(8,128)(2,1)} %table.1, ...), custom_call_target="tpu_custom_call" | custom-call | flops 32000000000 | bytes 60000000 | tf_op jit(solution)/shard_map/layer/pallas_call | solution.py:713
  155.1 4.7 %finish.1 = (bf16[2,256,768]{2,1,0:T(8,128)(2,1)}, f32[2,256,768]{2,1,0:T(8,128)}, f32[96,2304]{1,0:T(8,128)}, f32[96,768]{1,0:T(8,128)}, f32[96,3072]{1,0:T(8,1...) custom-call(bf16[2,256,768]{2,1,0:T(8,128)(2,1)} %get-tuple-element., ...), custom_call_target="tpu_custom_call" | custom-call | tf_op jit(solution)/shard_map/finish/pallas_call | solution.py:822

commit v4 on v3

--- a/solution.py
+++ b/solution.py
@@ -157,7 +157,7 @@
             self.step([(g.at[1 - b2, :, b0], r2, over_y)], [r2], lambda: self.fold_y(g, r2, b2, b0))
             self.step([(g.at[b2, 1 - b1, b0], r3, over_x)], [r3], lambda: add_into(own, r3))
         if kind[1] == "s":
-            slots = [r4.at[:, pl.ds(0, cols)], r4.at[:, pl.ds(cols, cols)], r5]
+            slots = [r4.at[:, pl.ds(0, cols)], r4.at[:, pl.ds(cols, cols)], r5.at[:, pl.ds(0, cols)]]
             there = [lax.rem(z + o, 4) for o in (1, 2, 3)]
             back = [lax.rem(z + 4 - o, 4) for o in (1, 2, 3)]
             moves = [(quarter(own, there[i]), slots[i], (d, there[i])) for i in range(3)]
@@ -165,19 +165,12 @@
             mine = quarter(self.out, z)
             self.step([(mine, mine, (d, one)) for one in there], [quarter(self.out, one) for one in back], None)
         else:
-            z0, z1 = lax.rem(z, 2), lax.div(z, 2)
+            z0 = lax.rem(z, 2)
             mine, other = at(z0, rows), at(1 - z0, rows)
-            left, right = at(z1, cols), at(1 - z1, cols)
-            half = own.at[mine]
+            half, done = own.at[mine], self.out.at[mine]
             one, two = (d, flip(z, 1)), (d, flip(z, 2))
             self.step([(own.at[other], r4, one)], [r4], lambda: add_into(half, r4))
-            self.step(
-                [(own.at[mine, right], r5, two)], [r5],
-                lambda: self.finish(own.at[mine, left], self.out.at[mine, left], [r5]),
-            )
-            done = self.out.at[mine, left]
-            self.step([(done, done, two)], [self.out.at[mine, right]], None)
-            done = self.out.at[mine]
+            self.step([(half, r5, two)], [r5], lambda: self.finish(half, done, [r5]))
             self.step([(done, done, one)], [self.out.at[other]], None)
 
     def step(self, moves, landing, combine):
@@ -241,43 +234,53 @@
                 copy.wait_send()
 
 
-KINDS = ("xs", "yh", "xh", "yh", "xh", "xs", "xh", "ys", "dh", "dh", "dh", "ds")
+KINDS = ("xs", "ye", "xe", "ye", "xs", "ys", "xe", "ye", "ds", "de", "de", "de")
 EARLY = 9
 UNITS = 12
 VECTORS, LOUT, GRAD = 12, 13, 15
 SCHEDULE = (
-    ((13, 0),),
-    ((0, 0), (14, 0)),
+    ((0, 0), (13, 0)),
     ((1, 0),),
     (),
     (),
     ((2, 0),),
     ((3, 0),),
     (),
-    (),
-    ((1, 1),),
-    ((0, 1),),
-    ((5, 0),),
+    ((14, 0),),
+    (),
+    ((1, 1), (0, 1)),
+    ((4, 0),),
     ((2, 1),),
-    ((7, 0),),
-    (),
-    ((0, 3), (3, 2)),
-    ((5, 2), (6, 0)),
-    ((7, 2), (10, 0)),
-    ((3, 4), (4, 2)),
-    ((1, 2), (0, 2), (3, 1)),
-    ((2, 2), (1, 3), (5, 1), (4, 0)),
-    ((2, 3), (1, 4), (7, 1)),
-    ((2, 4), (0, 4), (3, 3), (1, 5), (4, 1)),
-    ((5, 3), (2, 5), (1, 6)),
-    ((7, 3),),
-    ((15, 0), (2, 6), (5, 4), (3, 5), (4, 3), (6, 1)),
+    (),
+    ((1, 2), (5, 0)),
+    ((4, 1),),
+    ((4, 2), (0, 4)),
+    ((4, 3), (7, 1)),
+    ((5, 3), (9, 0)),
+    ((5, 4), (7, 3), (10, 0)),
+    ((0, 2), (3, 1)),
+    ((0, 3),),
+    ((8, 0), (3, 3)),
+    (),
+    ((7, 2), (8, 1), (3, 5), (4, 4)),
+    (),
+    (),
+    ((2, 3), (7, 0), (3, 2)),
+    ((1, 5), (2, 4)),
+    (),
+    (),
+    ((8, 2),),
+    ((2, 2), (1, 3), (6, 0)),
+    ((1, 4), (5, 1)),
+    ((5, 2),),
+    ((2, 5), (3, 4), (6, 1)),
+    ((6, 2),),
+    ((6, 3), (9, 1), (7, 4)),
+    ((15, 0), (8, 3), (11, 0)),
 )
 TAIL = (
-    (16, 0), (9, 0), (8, 0), (11, 0), (12, 0), (10, 1), (7, 4), (6, 2), (3, 6), (9, 1),
-    (4, 4), (8, 1), (10, 2), (6, 3), (9, 2), (4, 5), (12, 1), (8, 2), (11, 1), (10, 3),
-    (6, 4), (9, 3), (12, 2), (4, 6), (8, 3), (11, 2), (10, 4), (6, 5), (12, 3), (9, 4),
-    (8, 4), (10, 5), (11, 3), (6, 6), (9, 5), (12, 4), (8, 5),
+    (16, 0), (9, 2), (12, 0), (7, 5), (6, 4), (10, 1), (12, 1), (11, 1), (12, 2), (6, 5),
+    (10, 2), (11, 2), (9, 3), (12, 3), (10, 3), (9, 4), (11, 3), (10, 4), (12, 4), (11, 4),
 )
 HEAD_ROWS = 16
 STEP = 768
@@ -585,6 +588,8 @@
                 dvs.append(mm(probs.astype(BF), dout))
                 dks.append(mm(ds, q))
                 dqs.append(mm_tn(ds, kh))
+                if h == 0:
+                    points(PAIRS, p)
             return jnp.where(low_half, *dks), jnp.where(low_half, *dvs), dqs[0] + dqs[1]
 
         @pl.loop(0, PAIRS)
@@ -722,7 +727,7 @@
             vm((toks, width), BF), vm((toks, width), BF), vm((2, 16, width), BF), vm((2, 16, width), BF),
             vm((PAIRS, 2, 2 * toks, PAIR), BF), vm((PAIRS, 2, toks, PAIR), BF),
             vm((UNITS, 2, 2, shard, width), BF), vm((UNITS, 2, shard, width), BF), vm((UNITS, shard, width), BF),
-            vm((UNITS, shard // 2, width), BF), vm((UNITS, shard // 2, width // 2), BF),
+            vm((UNITS, shard // 2, width), BF), vm((UNITS, shard // 2, width), BF),
             vm((UNITS, shard, width), BF), vm((2, rows, width), F32), vm((stages, rows, width), F32),
             vm((toks, width), BF), vm((PAIRS, toks, PAIR), BF), vm((toks, width), BF), vm((toks, width), BF),
             vm((toks, width), F32), vm((toks, width), BF), vm((EARLY, 2, 2, 2, shard, width), BF),

time: 160 us -> 158 us (0.988)
  Pallas kernels: 159 us -> 157 us
    pallas_call x1, Pallas kernels: 154 us -> 152 us  [run_layer(): pl.pallas_call(functools.partial(layer_kernel, bits), out_shape=(sds((2,...]
where the time goes in v4:
time: 158 us; the launch traced here: 157 us
  Pallas kernels  157 us (99%)
    pallas_call x1, Pallas kernels, run_layer(): pl.pallas_call(functools.partial(layer_kernel, bits), out_shape=(sds((2,...  152 us
    pallas_call x1, Pallas kernels, run_finish(): pl.pallas_call(finish_kernel, out_shape=big + small, in_specs=[any_] * 4,...  4.7 us

profile of v4, /device:TPU:0, one launch (start us, length us, event | category | flops | bytes accessed | tf_op | source)
XLA Modules:
  0.0 157.4 jit_solution(8157212076880608883)
XLA Ops:
  0.6 151.8 %layer.1 = (bf16[2,256,768]{2,1,0:T(8,128)(2,1)}, bf16[2,256,768]{2,1,0:T(8,128)(2,1)}, bf16[12,96,768]{2,1,0:T(8,128)(2,1)}, f32[32,768]{1,0:T(8,128)}) custom-call(s32[2]{0:T(128)} %ts.1, s32[2]{0:T(128)} %buckets.1, bf16[2,256,768]{2,1,0:T(8,128)(2,1)} %x.1, bf16[2,256,768]{2,1,0:T(8,128)(2,1)} %cot.1, bf16[2000,768]{1,0:T(8,128)(2,1)} %table.1, ...), custom_call_target="tpu_custom_call" | custom-call | flops 32000000000 | bytes 60000000 | tf_op jit(solution)/shard_map/layer/pallas_call | solution.py:718
  152.5 4.7 %finish.1 = (bf16[2,256,768]{2,1,0:T(8,128)(2,1)}, f32[2,256,768]{2,1,0:T(8,128)}, f32[96,2304]{1,0:T(8,128)}, f32[96,768]{1,0:T(8,128)}, f32[96,3072]{1,0:T(8,1...) custom-call(bf16[2,256,768]{2,1,0:T(8,128)(2,1)} %get-tuple-element., ...), custom_call_target="tpu_custom_call" | custom-call | tf_op jit(solution)/shard_map/finish/pallas_call | solution.py:827
